TPU v7x, 32 devices: a whole 2x2x4 slice. The times are simulated.
32 devices in a mesh: tm: 4 (over y, x), space: 8 (over z, core).
Axes of the slice: x: 2, y: 2, z: 4, core: 2. Of those that a mesh axis runs over, the one named last changes fastest.
Arguments:
- starts: float32 [4, 64, 256, 128], P('tm', 'space'), may hold values from -6 to 6
- material: int32 [64, 256, 128], P('space'), may hold values from 0 to 7, as said below
- source: float32 [64, 256, 128], P('space'), may hold values from -6 to 6
Outputs:
- next_starts: float32 [4, 64, 256, 128], P('tm', 'space')
Inputs may be any that keep to these rules, and one draw needn't show every extreme that they name: `material`: index into the table of 8 conductivities.
All inputs are finite; a program needn't handle non-finite values.
Results may differ from a plain program's by a relative error of at most 0.0001.
Values sent between devices are 32-bit elements; how exact they have to be, the bound alone decides.
A program may use at most 64 MiB of HBM per device.

v0:
```python
import jax
import jax.numpy as jnp
from jax import lax
from jax.sharding import PartitionSpec as P

FSTEPS = 4
CSTEPS = 2
DEPTH = 2


conductivity_table = (1.0, 0.72, 0.52, 0.37, 0.26, 0.18, 0.13, 0.09)
fine_step = 0.15
coarse_step = 0.3


def with_halo(cells, sides, width):
    for axis, dim in sides:
        count = lax.axis_size(axis)
        ends = count - 1
        head = lax.slice_in_dim(cells, 0, width, axis=dim)
        tail = lax.slice_in_dim(cells, cells.shape[dim] - width, cells.shape[dim], axis=dim)
        cells = jnp.concatenate(
            [
                lax.ppermute(tail, axis, [(i, (i + 1) % count) for i in range(ends)]),
                cells,
                lax.ppermute(head, axis, [((i + 1) % count, i) for i in range(ends)]),
            ],
            axis=dim,
        )
    return cells


def shifted(x, axis, by):
    length = lax.axis_size(axis)
    pairs = [(i, i + by) for i in range(length) if 0 <= i + by < length]
    return lax.ppermute(x, axis, pairs)


def lookup(material):
    result = jnp.zeros(material.shape, jnp.float32)
    for number in range(8):
        result = jnp.where(material == number, jnp.float32(conductivity_table[number]), result)
    return result


def restrict(values):
    lead_dims = values.shape[:-3]
    folded = values.reshape(
        lead_dims + (values.shape[-3] // 2, 2, values.shape[-2] // 2, 2, values.shape[-1])
    )
    return jnp.mean(folded, axis=(-4, -2))


def prolong(values):
    lead_dims = values.shape[:-3]
    rows_x = values.shape[-3]
    rows_y = values.shape[-2]
    rows_z = values.shape[-1]
    spread = jnp.broadcast_to(
        values[..., :, None, :, None, :], lead_dims + (rows_x, 2, rows_y, 2, rows_z)
    )
    return spread.reshape(lead_dims + (rows_x * 2, rows_y * 2, rows_z))


def make_faces(cond_pad, weight_x, weight_y, weight_z):
    own = cond_pad[1:-1]
    face_x = weight_x * 0.5 * (cond_pad[1:] + cond_pad[:-1])
    pad_y = jnp.pad(own, ((0, 0), (1, 1), (0, 0)))
    face_y = weight_y * 0.5 * (pad_y[:, 1:] + pad_y[:, :-1])
    pad_z = jnp.pad(own, ((0, 0), (0, 0), (1, 1)))
    face_z = weight_z * 0.5 * (pad_z[:, :, 1:] + pad_z[:, :, :-1])
    return (face_x, face_y, face_z)


def diffuse(padded, face_x, face_y, face_z, source_in, step_size):
    current = padded[1:-1]
    grad_x = face_x * (padded[1:] - padded[:-1])
    flux = grad_x[1:] - grad_x[:-1]
    field_y = jnp.pad(current, ((0, 0), (1, 1), (0, 0)))
    grad_y = face_y * (field_y[:, 1:] - field_y[:, :-1])
    flux = flux + grad_y[:, 1:] - grad_y[:, :-1]
    field_z = jnp.pad(current, ((0, 0), (0, 0), (1, 1)))
    grad_z = face_z * (field_z[:, :, 1:] - field_z[:, :, :-1])
    flux = flux + grad_z[:, :, 1:] - grad_z[:, :, :-1]
    return current + step_size * (flux + source_in)


def local(starts, material, source):
    slab_index = lax.axis_index("tm")
    slab_count = lax.axis_size("tm")
    width_x = source.shape[0]
    conduct = lookup(material)
    coef_all = jnp.stack([conduct, source])
    coef_ext = with_halo(coef_all, (("space", 1),), DEPTH)
    ext_x, ext_y, ext_z = make_faces(coef_ext[0], 1.0, 1.0, 1.0)
    coarse_cond = restrict(coef_ext[0, DEPTH - 2 : DEPTH + width_x + 2])
    coarse_x, coarse_y, coarse_z = make_faces(coarse_cond, 0.25, 0.25, 1.0)
    coarse_source = restrict(source)
    near_x = ext_x[DEPTH - 1 : DEPTH + width_x]
    near_y = ext_y[DEPTH - 1 : DEPTH - 1 + width_x]
    near_z = ext_z[DEPTH - 1 : DEPTH - 1 + width_x]

    def coarse_run(current):
        reduced = restrict(current)
        for step_num in range(CSTEPS):
            padded = with_halo(reduced, (("space", 0),), 1)
            reduced = diffuse(padded, coarse_x, coarse_y, coarse_z, coarse_source, coarse_step)
        return reduced

    current = starts[0]
    coarse_now = prolong(coarse_run(current))
    fine_current = current
    for step_num in range(FSTEPS):
        padded = with_halo(fine_current, (("space", 0),), 1)
        fine_current = diffuse(padded, near_x, near_y, near_z, source, fine_step)
    offset = fine_current - coarse_now
    chain_start = current
    offset_left = shifted(offset, "tm", 1)
    for round_num in range(slab_count - 1):
        arrived = shifted(coarse_run(chain_start), "tm", 1)
        chain_start = jnp.where(slab_index > round_num, prolong(arrived) + offset_left, chain_start)
    current = chain_start
    coarse_now = prolong(coarse_run(current))
    last_end = coarse_now + offset
    newest = shifted(last_end, "tm", 1 - slab_count)
    return jnp.where(slab_index == 0, newest, current)[None]


def solution(mesh):
    in_specs = (P("tm", "space", None, None), P("space", None, None), P("space", None, None))
    out_specs = P("tm", "space", None, None)
    return jax.shard_map(local, mesh=mesh, in_specs=in_specs, out_specs=out_specs, check_vma=False)
```

profile of v0, /device:TPU:1, one launch (start us, length us, event | category | flops | bytes accessed | tf_op | source)
XLA Modules:
  0.0 220.9 jit_solution(12238415952892430529)
XLA Ops:
  3.0 4.6 %collective-permute-start = (f32[2,2,256,128]{3,2,1,0:T(8,128)}, f32[2,2,256,128]{3,2,1,0:T(8,128)}, u32[]{:S(2)}, u32[]{:S(2)}) collective-permute-start(f32[2,2,256,128]{3,2,1,0:T(8,128)} %get-tuple-element.19), channel_id=1, source_target_pairs={{0,1},{1,2},{2,3},{3,4},{4,5},{5,6},{6,7},{8,9},{9,10},{10,11},{11... | collective-permute-start | bytes 1572872 | tf_op jit(solution)/shard_map/ppermute | solution.py:24
  7.5 1.9 collective-permute-start.1
  12.2 3.6 %collective-permute-start.8 = (f32[1,256,128]{2,1,0:T(8,128)}, f32[1,256,128]{2,1,0:T(8,128)}, u32[]{:S(2)}, u32[]{:S(2)}) collective-permute-start(f32[1,256,128]{2,1,0:T(8,128)} %get-tuple-element.31), channel_id=1, source_target_pairs={{0,1},{1,2},{2,3},{3,4},{4,5},{5,6},{6,7},{8,9},{9,10},{10,11},{11... | collective-permute-start | bytes 393224 | tf_op jit(solution)/shard_map/ppermute | solution.py:24
  21.7 3.6 %collective-permute-start.3 = (f32[1,128,128]{2,1,0:T(8,128)S(1)}, f32[1,128,128]{2,1,0:T(8,128)}, u32[]{:S(2)}, u32[]{:S(2)}) collective-permute-start(f32[1,128,128]{2,1,0:T(8,128)S(1)} %get-tuple-element.47), channel_id=1, source_target_pairs={{0,1},{1,2},{2,3},{3,4},{4,5},{5,6},{6,7},{8,9},{9,10},{10,11},{11... | collective-permute-start | bytes 196616 | tf_op jit(solution)/shard_map/ppermute | solution.py:24
  30.9 2.3 %fusion.11 = (f32[9,256,128]{2,1,0:T(8,128)S(1)}, f32[9,256,128]{2,1,0:T(8,128)}) fusion(f32[1,256,128]{2,1,0:T(8,128)} %collective-permute-done.7, f32[8,256,128]{2,1,0:T(8,128)S(1)} %bitcast.34, f32[1,256,128]{2,1,0:T(8,128)} %collective-permute-done.8, f32[1,11,256,128]{3,2,1,0:T(8,128)S(1)} %get-tuple-element.18, ...), kind=kLoop, calls=%fused_computation.28 | loop fusion | flops 1769472 | bytes 6029312 | tf_op jit(solution)/shard_map/mul | solution.py:77
  36.5 3.0 %collective-permute-start.9 = (f32[1,256,128]{2,1,0:T(8,128)}, f32[1,256,128]{2,1,0:T(8,128)}, u32[]{:S(2)}, u32[]{:S(2)}) collective-permute-start(f32[1,256,128]{2,1,0:T(8,128)} %get-tuple-element.30), channel_id=1, source_target_pairs={{1,0},{2,1},{3,2},{4,3},{5,4},{6,5},{7,6},{9,8},{10,9},{11,10},{12... | collective-permute-start | bytes 393224 | tf_op jit(solution)/shard_map/ppermute | solution.py:26
  40.8 1.9 fusion.3
  42.8 2.6 %reduce_sum.59 = f32[6,128,128]{2,1,0:T(8,128)S(1)} reduce(f32[6,2,128,2,128]{4,3,2,1,0:T(2,128)} %bitcast.38, f32[]{:T(128)} %constant.27.clone.1), dimensions={1,3}, to_apply=%region_1.2 | reduce | flops 294912 | bytes 1966084 | tf_op jit(solution)/shard_map/reduce_sum | solution.py:51
  47.5 1.9 collective-permute-start.4
  49.4 3.6 %collective-permute-start.5 = (f32[1,128,128]{2,1,0:T(8,128)S(1)}, f32[1,128,128]{2,1,0:T(8,128)S(1)}, u32[]{:S(2)}, u32[]{:S(2)}) collective-permute-start(f32[1,128,128]{2,1,0:T(8,128)S(1)} %get-tuple-element.45), channel_id=1, source_target_pairs={{0,1},{1,2},{2,3},{3,4},{4,5},{5,6},{6,7},{8,9},{9,10},{10,11},{11... | collective-permute-start | bytes 196616 | tf_op jit(solution)/shard_map/ppermute | solution.py:24
  62.3 4.4 %collective-permute-start.12 = (f32[1,256,128]{2,1,0:T(8,128)S(1)}, f32[1,256,128]{2,1,0:T(8,128)S(1)}, u32[]{:S(2)}, u32[]{:S(2)}) collective-permute-start(f32[1,256,128]{2,1,0:T(8,128)S(1)} %get-tuple-element.27), channel_id=1, source_target_pairs={{0,1},{1,2},{2,3},{3,4},{4,5},{5,6},{6,7},{8,9},{9,10},{10,11},{11... | collective-permute-start | bytes 393224 | tf_op jit(solution)/shard_map/ppermute | solution.py:24
  71.8 4.4 %collective-permute-start.14 = (f32[1,256,128]{2,1,0:T(8,128)S(1)}, f32[1,256,128]{2,1,0:T(8,128)S(1)}, u32[]{:S(2)}, u32[]{:S(2)}) collective-permute-start(f32[1,256,128]{2,1,0:T(8,128)S(1)} %get-tuple-element.25), channel_id=1, source_target_pairs={{0,1},{1,2},{2,3},{3,4},{4,5},{5,6},{6,7},{8,9},{9,10},{10,11},{11... | collective-permute-start | bytes 393224 | tf_op jit(solution)/shard_map/ppermute | solution.py:24
  81.0 3.2 %collective-permute-start.15 = (f32[8,256,128]{2,1,0:T(8,128)}, f32[8,256,128]{2,1,0:T(8,128)S(1)}, u32[]{:S(2)}, u32[]{:S(2)}) collective-permute-start(f32[8,256,128]{2,1,0:T(8,128)} %fusion.19), channel_id=1, source_target_pairs={{0,8},{8,16},{16,24},{1,9},{9,17},{17,25},{2,10},{10,18},{18,26},{... | collective-permute-start | bytes 3145736 | tf_op jit(solution)/shard_map/ppermute | solution.py:36
  84.1 3.8 %collective-permute-start.6 = (f32[4,128,128]{2,1,0:T(8,128)}, f32[4,128,128]{2,1,0:T(8,128)}, u32[]{:S(2)}, u32[]{:S(2)}) collective-permute-start(f32[4,128,128]{2,1,0:T(8,128)} %fusion.76), channel_id=1, source_target_pairs={{0,8},{8,16},{16,24},{1,9},{9,17},{17,25},{2,10},{10,18},{18,26},{... | collective-permute-start | bytes 786440 | tf_op jit(solution)/shard_map/ppermute | solution.py:36
  87.9 22.6 %collective-permute-done.6 = f32[4,128,128]{2,1,0:T(8,128)} collective-permute-done((f32[4,128,128]{2,1,0:T(8,128)}, f32[4,128,128]{2,1,0:T(8,128)}, u32[]{:S(2)}, u32[]{:S(2)}) %collective-permute-start.6) | collective-permute-done | bytes 262176 | tf_op jit(solution)/shard_map/ppermute | solution.py:36
  113.0 2.0 reduce_sum.61
  117.1 5.3 %collective-permute-start.17 = (f32[1,128,128]{2,1,0:T(8,128)S(1)}, f32[1,128,128]{2,1,0:T(8,128)S(1)}, u32[]{:S(2)}, u32[]{:S(2)}) collective-permute-start(f32[1,128,128]{2,1,0:T(8,128)S(1)} %get-tuple-element.43), channel_id=1, source_target_pairs={{0,1},{1,2},{2,3},{3,4},{4,5},{5,6},{6,7},{8,9},{9,10},{10,11},{11... | collective-permute-start | bytes 196616 | tf_op jit(solution)/shard_map/ppermute | solution.py:24
  124.2 1.9 collective-permute-start.18
  126.1 4.3 %collective-permute-start.19 = (f32[1,128,128]{2,1,0:T(8,128)S(1)}, f32[1,128,128]{2,1,0:T(8,128)S(1)}, u32[]{:S(2)}, u32[]{:S(2)}) collective-permute-start(f32[1,128,128]{2,1,0:T(8,128)S(1)} %get-tuple-element.41), channel_id=1, source_target_pairs={{0,1},{1,2},{2,3},{3,4},{4,5},{5,6},{6,7},{8,9},{9,10},{10,11},{11... | collective-permute-start | bytes 196616 | tf_op jit(solution)/shard_map/ppermute | solution.py:24
  132.6 4.1 %collective-permute-start.20 = (f32[4,128,128]{2,1,0:T(8,128)}, f32[4,128,128]{2,1,0:T(8,128)S(1)}, u32[]{:S(2)}, u32[]{:S(2)}) collective-permute-start(f32[4,128,128]{2,1,0:T(8,128)} %fusion.70), channel_id=1, source_target_pairs={{0,8},{8,16},{16,24},{1,9},{9,17},{17,25},{2,10},{10,18},{18,26},{... | collective-permute-start | bytes 786440 | tf_op jit(solution)/shard_map/ppermute | solution.py:36
  136.8 4.6 %collective-permute-done.20 = f32[4,128,128]{2,1,0:T(8,128)S(1)} collective-permute-done((f32[4,128,128]{2,1,0:T(8,128)}, f32[4,128,128]{2,1,0:T(8,128)S(1)}, u32[]{:S(2)}, u32[]{:S(2)}) %collective-permute-start.20) | collective-permute-done | bytes 262176 | tf_op jit(solution)/shard_map/ppermute | solution.py:36
  145.8 2.1 collective-permute-start.21
  147.9 5.3 %collective-permute-start.22 = (f32[1,128,128]{2,1,0:T(8,128)S(1)}, f32[1,128,128]{2,1,0:T(8,128)S(1)}, u32[]{:S(2)}, u32[]{:S(2)}) collective-permute-start(f32[1,128,128]{2,1,0:T(8,128)S(1)} %get-tuple-element.39), channel_id=1, source_target_pairs={{0,1},{1,2},{2,3},{3,4},{4,5},{5,6},{6,7},{8,9},{9,10},{10,11},{11... | collective-permute-start | bytes 196616 | tf_op jit(solution)/shard_map/ppermute | solution.py:24
  155.0 1.9 collective-permute-start.23
  156.9 4.3 %collective-permute-start.24 = (f32[1,128,128]{2,1,0:T(8,128)S(1)}, f32[1,128,128]{2,1,0:T(8,128)S(1)}, u32[]{:S(2)}, u32[]{:S(2)}) collective-permute-start(f32[1,128,128]{2,1,0:T(8,128)S(1)} %get-tuple-element.37), channel_id=1, source_target_pairs={{0,1},{1,2},{2,3},{3,4},{4,5},{5,6},{6,7},{8,9},{9,10},{10,11},{11... | collective-permute-start | bytes 196616 | tf_op jit(solution)/shard_map/ppermute | solution.py:24
  163.4 4.7 %collective-permute-start.25 = (f32[4,128,128]{2,1,0:T(8,128)}, f32[4,128,128]{2,1,0:T(8,128)}, u32[]{:S(2)}, u32[]{:S(2)}) collective-permute-start(f32[4,128,128]{2,1,0:T(8,128)} %fusion.64), channel_id=1, source_target_pairs={{0,8},{8,16},{16,24},{1,9},{9,17},{17,25},{2,10},{10,18},{18,26},{... | collective-permute-start | bytes 786440 | tf_op jit(solution)/shard_map/ppermute | solution.py:36
  168.1 3.9 %collective-permute-done.25 = f32[4,128,128]{2,1,0:T(8,128)} collective-permute-done((f32[4,128,128]{2,1,0:T(8,128)}, f32[4,128,128]{2,1,0:T(8,128)}, u32[]{:S(2)}, u32[]{:S(2)}) %collective-permute-start.25) | collective-permute-done | bytes 262176 | tf_op jit(solution)/shard_map/ppermute | solution.py:36
  174.5 2.0 reduce_sum.63
  178.6 4.1 %collective-permute-start.27 = (f32[1,128,128]{2,1,0:T(8,128)S(1)}, f32[1,128,128]{2,1,0:T(8,128)S(1)}, u32[]{:S(2)}, u32[]{:S(2)}) collective-permute-start(f32[1,128,128]{2,1,0:T(8,128)S(1)} %get-tuple-element.35), channel_id=1, source_target_pairs={{0,1},{1,2},{2,3},{3,4},{4,5},{5,6},{6,7},{8,9},{9,10},{10,11},{11... | collective-permute-start | bytes 196616 | tf_op jit(solution)/shard_map/ppermute | solution.py:24
  184.5 1.9 collective-permute-start.28
  186.5 4.3 %collective-permute-start.29 = (f32[1,128,128]{2,1,0:T(8,128)S(1)}, f32[1,128,128]{2,1,0:T(8,128)S(1)}, u32[]{:S(2)}, u32[]{:S(2)}) collective-permute-start(f32[1,128,128]{2,1,0:T(8,128)S(1)} %get-tuple-element.33), channel_id=1, source_target_pairs={{0,1},{1,2},{2,3},{3,4},{4,5},{5,6},{6,7},{8,9},{9,10},{10,11},{11... | collective-permute-start | bytes 196616 | tf_op jit(solution)/shard_map/ppermute | solution.py:24
  195.3 24.6 %collective-permute-done.30 = f32[8,256,128]{2,1,0:T(8,128)S(1)} collective-permute-done((f32[8,256,128]{2,1,0:T(8,128)S(1)}, f32[8,256,128]{2,1,0:T(8,128)S(1)}, u32[]{:S(2)}, u32[]{:S(2)}) %collective-permute-start.30) | collective-permute-done | bytes 1048608 | tf_op jit(solution)/shard_map/ppermute | solution.py:36
  (154 shorter events, 71.3 us)
Async XLA Ops:
  3.0 18.8 %collective-permute-start = (f32[2,2,256,128]{3,2,1,0:T(8,128)}, f32[2,2,256,128]{3,2,1,0:T(8,128)}, u32[]{:S(2)}, u32[]{:S(2)}) collective-permute-start(f32[2,2,256,128]{3,2,1,0:T(8,128)} %get-tuple-element.19), channel_id=1, source_target_pairs={{0,1},{1,2},{2,3},{3,4},{4,5},{5,6},{6,7},{8,9},{9,10},{10,11},{11... | collective-permute-start | bytes 1572872 | tf_op jit(solution)/shard_map/ppermute | solution.py:24
  7.5 17.8 %collective-permute-start.1 = (f32[2,2,256,128]{3,2,1,0:T(8,128)}, f32[2,2,256,128]{3,2,1,0:T(8,128)}, u32[]{:S(2)}, u32[]{:S(2)}) collective-permute-start(f32[2,2,256,128]{3,2,1,0:T(8,128)} %get-tuple-element.20), channel_id=1, source_target_pairs={{1,0},{2,1},{3,2},{4,3},{5,4},{6,5},{7,6},{9,8},{10,9},{11,10},{12... | collective-permute-start | bytes 1572872 | tf_op jit(solution)/shard_map/ppermute | solution.py:26
  10.2 20.7 %collective-permute-start.7 = (f32[1,256,128]{2,1,0:T(8,128)}, f32[1,256,128]{2,1,0:T(8,128)}, u32[]{:S(2)}, u32[]{:S(2)}) collective-permute-start(f32[1,256,128]{2,1,0:T(8,128)} %get-tuple-element.32), channel_id=1, source_target_pairs={{1,0},{2,1},{3,2},{4,3},{5,4},{6,5},{7,6},{9,8},{10,9},{11,10},{12... | collective-permute-start | bytes 393224 | tf_op jit(solution)/shard_map/ppermute | solution.py:26
  12.2 18.8 %collective-permute-start.8 = (f32[1,256,128]{2,1,0:T(8,128)}, f32[1,256,128]{2,1,0:T(8,128)}, u32[]{:S(2)}, u32[]{:S(2)}) collective-permute-start(f32[1,256,128]{2,1,0:T(8,128)} %get-tuple-element.31), channel_id=1, source_target_pairs={{0,1},{1,2},{2,3},{3,4},{4,5},{5,6},{6,7},{8,9},{9,10},{10,11},{11... | collective-permute-start | bytes 393224 | tf_op jit(solution)/shard_map/ppermute | solution.py:24
  19.0 26.8 %collective-permute-start.2 = (f32[1,128,128]{2,1,0:T(8,128)}, f32[1,128,128]{2,1,0:T(8,128)}, u32[]{:S(2)}, u32[]{:S(2)}) collective-permute-start(f32[1,128,128]{2,1,0:T(8,128)} %get-tuple-element.48), channel_id=1, source_target_pairs={{1,0},{2,1},{3,2},{4,3},{5,4},{6,5},{7,6},{9,8},{10,9},{11,10},{12... | collective-permute-start | bytes 196616 | tf_op jit(solution)/shard_map/ppermute | solution.py:26
  21.7 24.2 %collective-permute-start.3 = (f32[1,128,128]{2,1,0:T(8,128)S(1)}, f32[1,128,128]{2,1,0:T(8,128)}, u32[]{:S(2)}, u32[]{:S(2)}) collective-permute-start(f32[1,128,128]{2,1,0:T(8,128)S(1)} %get-tuple-element.47), channel_id=1, source_target_pairs={{0,1},{1,2},{2,3},{3,4},{4,5},{5,6},{6,7},{8,9},{9,10},{10,11},{11... | collective-permute-start | bytes 196616 | tf_op jit(solution)/shard_map/ppermute | solution.py:24
  34.6 20.8 %collective-permute-start.10 = (f32[1,256,128]{2,1,0:T(8,128)}, f32[1,256,128]{2,1,0:T(8,128)}, u32[]{:S(2)}, u32[]{:S(2)}) collective-permute-start(f32[1,256,128]{2,1,0:T(8,128)} %get-tuple-element.29), channel_id=1, source_target_pairs={{0,1},{1,2},{2,3},{3,4},{4,5},{5,6},{6,7},{8,9},{9,10},{10,11},{11... | collective-permute-start | bytes 393224 | tf_op jit(solution)/shard_map/ppermute | solution.py:24
  36.5 18.9 %collective-permute-start.9 = (f32[1,256,128]{2,1,0:T(8,128)}, f32[1,256,128]{2,1,0:T(8,128)}, u32[]{:S(2)}, u32[]{:S(2)}) collective-permute-start(f32[1,256,128]{2,1,0:T(8,128)} %get-tuple-element.30), channel_id=1, source_target_pairs={{1,0},{2,1},{3,2},{4,3},{5,4},{6,5},{7,6},{9,8},{10,9},{11,10},{12... | collective-permute-start | bytes 393224 | tf_op jit(solution)/shard_map/ppermute | solution.py:26
  47.5 5.8 %collective-permute-start.4 = (f32[1,128,128]{2,1,0:T(8,128)S(1)}, f32[1,128,128]{2,1,0:T(8,128)S(1)}, u32[]{:S(2)}, u32[]{:S(2)}) collective-permute-start(f32[1,128,128]{2,1,0:T(8,128)S(1)} %get-tuple-element.46), channel_id=1, source_target_pairs={{1,0},{2,1},{3,2},{4,3},{5,4},{6,5},{7,6},{9,8},{10,9},{11,10},{12... | collective-permute-start | bytes 196616 | tf_op jit(solution)/shard_map/ppermute | solution.py:26
  49.4 5.0 %collective-permute-start.5 = (f32[1,128,128]{2,1,0:T(8,128)S(1)}, f32[1,128,128]{2,1,0:T(8,128)S(1)}, u32[]{:S(2)}, u32[]{:S(2)}) collective-permute-start(f32[1,128,128]{2,1,0:T(8,128)S(1)} %get-tuple-element.45), channel_id=1, source_target_pairs={{0,1},{1,2},{2,3},{3,4},{4,5},{5,6},{6,7},{8,9},{9,10},{10,11},{11... | collective-permute-start | bytes 196616 | tf_op jit(solution)/shard_map/ppermute | solution.py:24
  60.4 6.9 %collective-permute-start.11 = (f32[1,256,128]{2,1,0:T(8,128)S(1)}, f32[1,256,128]{2,1,0:T(8,128)S(1)}, u32[]{:S(2)}, u32[]{:S(2)}) collective-permute-start(f32[1,256,128]{2,1,0:T(8,128)S(1)} %get-tuple-element.28), channel_id=1, source_target_pairs={{1,0},{2,1},{3,2},{4,3},{5,4},{6,5},{7,6},{9,8},{10,9},{11,10},{12... | collective-permute-start | bytes 393224 | tf_op jit(solution)/shard_map/ppermute | solution.py:26
  62.3 6.2 %collective-permute-start.12 = (f32[1,256,128]{2,1,0:T(8,128)S(1)}, f32[1,256,128]{2,1,0:T(8,128)S(1)}, u32[]{:S(2)}, u32[]{:S(2)}) collective-permute-start(f32[1,256,128]{2,1,0:T(8,128)S(1)} %get-tuple-element.27), channel_id=1, source_target_pairs={{0,1},{1,2},{2,3},{3,4},{4,5},{5,6},{6,7},{8,9},{9,10},{10,11},{11... | collective-permute-start | bytes 393224 | tf_op jit(solution)/shard_map/ppermute | solution.py:24
  69.8 7.0 %collective-permute-start.13 = (f32[1,256,128]{2,1,0:T(8,128)S(1)}, f32[1,256,128]{2,1,0:T(8,128)S(1)}, u32[]{:S(2)}, u32[]{:S(2)}) collective-permute-start(f32[1,256,128]{2,1,0:T(8,128)S(1)} %get-tuple-element.26), channel_id=1, source_target_pairs={{1,0},{2,1},{3,2},{4,3},{5,4},{6,5},{7,6},{9,8},{10,9},{11,10},{12... | collective-permute-start | bytes 393224 | tf_op jit(solution)/shard_map/ppermute | solution.py:26
  71.8 6.3 %collective-permute-start.14 = (f32[1,256,128]{2,1,0:T(8,128)S(1)}, f32[1,256,128]{2,1,0:T(8,128)S(1)}, u32[]{:S(2)}, u32[]{:S(2)}) collective-permute-start(f32[1,256,128]{2,1,0:T(8,128)S(1)} %get-tuple-element.25), channel_id=1, source_target_pairs={{0,1},{1,2},{2,3},{3,4},{4,5},{5,6},{6,7},{8,9},{9,10},{10,11},{11... | collective-permute-start | bytes 393224 | tf_op jit(solution)/shard_map/ppermute | solution.py:24
  81.0 29.6 %collective-permute-start.15 = (f32[8,256,128]{2,1,0:T(8,128)}, f32[8,256,128]{2,1,0:T(8,128)S(1)}, u32[]{:S(2)}, u32[]{:S(2)}) collective-permute-start(f32[8,256,128]{2,1,0:T(8,128)} %fusion.19), channel_id=1, source_target_pairs={{0,8},{8,16},{16,24},{1,9},{9,17},{17,25},{2,10},{10,18},{18,26},{... | collective-permute-start | bytes 3145736 | tf_op jit(solution)/shard_map/ppermute | solution.py:36
  84.1 26.4 %collective-permute-start.6 = (f32[4,128,128]{2,1,0:T(8,128)}, f32[4,128,128]{2,1,0:T(8,128)}, u32[]{:S(2)}, u32[]{:S(2)}) collective-permute-start(f32[4,128,128]{2,1,0:T(8,128)} %fusion.76), channel_id=1, source_target_pairs={{0,8},{8,16},{16,24},{1,9},{9,17},{17,25},{2,10},{10,18},{18,26},{... | collective-permute-start | bytes 786440 | tf_op jit(solution)/shard_map/ppermute | solution.py:36
  115.2 7.3 %collective-permute-start.16 = (f32[1,128,128]{2,1,0:T(8,128)S(1)}, f32[1,128,128]{2,1,0:T(8,128)S(1)}, u32[]{:S(2)}, u32[]{:S(2)}) collective-permute-start(f32[1,128,128]{2,1,0:T(8,128)S(1)} %get-tuple-element.44), channel_id=1, source_target_pairs={{1,0},{2,1},{3,2},{4,3},{5,4},{6,5},{7,6},{9,8},{10,9},{11,10},{12... | collective-permute-start | bytes 196616 | tf_op jit(solution)/shard_map/ppermute | solution.py:26
  117.1 6.6 %collective-permute-start.17 = (f32[1,128,128]{2,1,0:T(8,128)S(1)}, f32[1,128,128]{2,1,0:T(8,128)S(1)}, u32[]{:S(2)}, u32[]{:S(2)}) collective-permute-start(f32[1,128,128]{2,1,0:T(8,128)S(1)} %get-tuple-element.43), channel_id=1, source_target_pairs={{0,1},{1,2},{2,3},{3,4},{4,5},{5,6},{6,7},{8,9},{9,10},{10,11},{11... | collective-permute-start | bytes 196616 | tf_op jit(solution)/shard_map/ppermute | solution.py:24
  124.2 6.3 %collective-permute-start.18 = (f32[1,128,128]{2,1,0:T(8,128)S(1)}, f32[1,128,128]{2,1,0:T(8,128)S(1)}, u32[]{:S(2)}, u32[]{:S(2)}) collective-permute-start(f32[1,128,128]{2,1,0:T(8,128)S(1)} %get-tuple-element.42), channel_id=1, source_target_pairs={{1,0},{2,1},{3,2},{4,3},{5,4},{6,5},{7,6},{9,8},{10,9},{11,10},{12... | collective-permute-start | bytes 196616 | tf_op jit(solution)/shard_map/ppermute | solution.py:26
  126.1 5.6 %collective-permute-start.19 = (f32[1,128,128]{2,1,0:T(8,128)S(1)}, f32[1,128,128]{2,1,0:T(8,128)S(1)}, u32[]{:S(2)}, u32[]{:S(2)}) collective-permute-start(f32[1,128,128]{2,1,0:T(8,128)S(1)} %get-tuple-element.41), channel_id=1, source_target_pairs={{0,1},{1,2},{2,3},{3,4},{4,5},{5,6},{6,7},{8,9},{9,10},{10,11},{11... | collective-permute-start | bytes 196616 | tf_op jit(solution)/shard_map/ppermute | solution.py:24
  132.6 8.7 %collective-permute-start.20 = (f32[4,128,128]{2,1,0:T(8,128)}, f32[4,128,128]{2,1,0:T(8,128)S(1)}, u32[]{:S(2)}, u32[]{:S(2)}) collective-permute-start(f32[4,128,128]{2,1,0:T(8,128)} %fusion.70), channel_id=1, source_target_pairs={{0,8},{8,16},{16,24},{1,9},{9,17},{17,25},{2,10},{10,18},{18,26},{... | collective-permute-start | bytes 786440 | tf_op jit(solution)/shard_map/ppermute | solution.py:36
  145.8 7.4 %collective-permute-start.21 = (f32[1,128,128]{2,1,0:T(8,128)S(1)}, f32[1,128,128]{2,1,0:T(8,128)S(1)}, u32[]{:S(2)}, u32[]{:S(2)}) collective-permute-start(f32[1,128,128]{2,1,0:T(8,128)S(1)} %get-tuple-element.40), channel_id=1, source_target_pairs={{1,0},{2,1},{3,2},{4,3},{5,4},{6,5},{7,6},{9,8},{10,9},{11,10},{12... | collective-permute-start | bytes 196616 | tf_op jit(solution)/shard_map/ppermute | solution.py:26
  147.9 6.6 %collective-permute-start.22 = (f32[1,128,128]{2,1,0:T(8,128)S(1)}, f32[1,128,128]{2,1,0:T(8,128)S(1)}, u32[]{:S(2)}, u32[]{:S(2)}) collective-permute-start(f32[1,128,128]{2,1,0:T(8,128)S(1)} %get-tuple-element.39), channel_id=1, source_target_pairs={{0,1},{1,2},{2,3},{3,4},{4,5},{5,6},{6,7},{8,9},{9,10},{10,11},{11... | collective-permute-start | bytes 196616 | tf_op jit(solution)/shard_map/ppermute | solution.py:24
  155.0 6.3 %collective-permute-start.23 = (f32[1,128,128]{2,1,0:T(8,128)S(1)}, f32[1,128,128]{2,1,0:T(8,128)S(1)}, u32[]{:S(2)}, u32[]{:S(2)}) collective-permute-start(f32[1,128,128]{2,1,0:T(8,128)S(1)} %get-tuple-element.38), channel_id=1, source_target_pairs={{1,0},{2,1},{3,2},{4,3},{5,4},{6,5},{7,6},{9,8},{10,9},{11,10},{12... | collective-permute-start | bytes 196616 | tf_op jit(solution)/shard_map/ppermute | solution.py:26
  156.9 5.6 %collective-permute-start.24 = (f32[1,128,128]{2,1,0:T(8,128)S(1)}, f32[1,128,128]{2,1,0:T(8,128)S(1)}, u32[]{:S(2)}, u32[]{:S(2)}) collective-permute-start(f32[1,128,128]{2,1,0:T(8,128)S(1)} %get-tuple-element.37), channel_id=1, source_target_pairs={{0,1},{1,2},{2,3},{3,4},{4,5},{5,6},{6,7},{8,9},{9,10},{10,11},{11... | collective-permute-start | bytes 196616 | tf_op jit(solution)/shard_map/ppermute | solution.py:24
  163.4 8.6 %collective-permute-start.25 = (f32[4,128,128]{2,1,0:T(8,128)}, f32[4,128,128]{2,1,0:T(8,128)}, u32[]{:S(2)}, u32[]{:S(2)}) collective-permute-start(f32[4,128,128]{2,1,0:T(8,128)} %fusion.64), channel_id=1, source_target_pairs={{0,8},{8,16},{16,24},{1,9},{9,17},{17,25},{2,10},{10,18},{18,26},{... | collective-permute-start | bytes 786440 | tf_op jit(solution)/shard_map/ppermute | solution.py:36
  176.7 6.1 %collective-permute-start.26 = (f32[1,128,128]{2,1,0:T(8,128)S(1)}, f32[1,128,128]{2,1,0:T(8,128)S(1)}, u32[]{:S(2)}, u32[]{:S(2)}) collective-permute-start(f32[1,128,128]{2,1,0:T(8,128)S(1)} %get-tuple-element.36), channel_id=1, source_target_pairs={{1,0},{2,1},{3,2},{4,3},{5,4},{6,5},{7,6},{9,8},{10,9},{11,10},{12... | collective-permute-start | bytes 196616 | tf_op jit(solution)/shard_map/ppermute | solution.py:26
  178.6 5.4 %collective-permute-start.27 = (f32[1,128,128]{2,1,0:T(8,128)S(1)}, f32[1,128,128]{2,1,0:T(8,128)S(1)}, u32[]{:S(2)}, u32[]{:S(2)}) collective-permute-start(f32[1,128,128]{2,1,0:T(8,128)S(1)} %get-tuple-element.35), channel_id=1, source_target_pairs={{0,1},{1,2},{2,3},{3,4},{4,5},{5,6},{6,7},{8,9},{9,10},{10,11},{11... | collective-permute-start | bytes 196616 | tf_op jit(solution)/shard_map/ppermute | solution.py:24
  184.5 6.3 %collective-permute-start.28 = (f32[1,128,128]{2,1,0:T(8,128)S(1)}, f32[1,128,128]{2,1,0:T(8,128)S(1)}, u32[]{:S(2)}, u32[]{:S(2)}) collective-permute-start(f32[1,128,128]{2,1,0:T(8,128)S(1)} %get-tuple-element.34), channel_id=1, source_target_pairs={{1,0},{2,1},{3,2},{4,3},{5,4},{6,5},{7,6},{9,8},{10,9},{11,10},{12... | collective-permute-start | bytes 196616 | tf_op jit(solution)/shard_map/ppermute | solution.py:26
  186.5 5.6 %collective-permute-start.29 = (f32[1,128,128]{2,1,0:T(8,128)S(1)}, f32[1,128,128]{2,1,0:T(8,128)S(1)}, u32[]{:S(2)}, u32[]{:S(2)}) collective-permute-start(f32[1,128,128]{2,1,0:T(8,128)S(1)} %get-tuple-element.33), channel_id=1, source_target_pairs={{0,1},{1,2},{2,3},{3,4},{4,5},{5,6},{6,7},{8,9},{9,10},{10,11},{11... | collective-permute-start | bytes 196616 | tf_op jit(solution)/shard_map/ppermute | solution.py:24
  192.5 27.3 %copy-start.9 = (f32[8,256,128]{2,1,0:T(8,128)S(1)}, f32[8,256,128]{2,1,0:T(8,128)}, u32[]{:S(2)}) copy-start(f32[8,256,128]{2,1,0:T(8,128)} %add_select_fusion) | copy-start | bytes 3145732
  194.0 25.9 %collective-permute-start.30 = (f32[8,256,128]{2,1,0:T(8,128)S(1)}, f32[8,256,128]{2,1,0:T(8,128)S(1)}, u32[]{:S(2)}, u32[]{:S(2)}) collective-permute-start(f32[8,256,128]{2,1,0:T(8,128)S(1)} %add.296), channel_id=1, source_target_pairs={{24,0},{25,1},{26,2},{27,3},{28,4},{29,5},{30,6},{31,7}} | collective-permute-start | bytes 3145736 | tf_op jit(solution)/shard_map/ppermute | solution.py:36
  (16 other events, 69.9 us)
where the time goes:
time: 222 us; the launch traced here: 221 us
  starting transfers between devices  97 us (44%)
  waiting for transfers between devices  67.6 us (30%)
  other arithmetic  42.7 us (19%)
  local copies, waits for them, and re-layouts  12.7 us (6%)
    ppermute x5, waiting for transfers between devices, shifted(): return lax.ppermute(x, axis, pairs)  55.7 us
    ppermute x13, starting transfers between devices, with_halo(): lax.ppermute(tail, axis, [(i, (i + 1) % count) for i in range(ends)])  53.8 us
    ppermute x13, starting transfers between devices, with_halo(): lax.ppermute(head, axis, [((i + 1) % count, i) for i in range(ends)])  26.2 us
    ppermute x5, starting transfers between devices, shifted(): return lax.ppermute(x, axis, pairs)  17 us
    ppermute x13, waiting for transfers between devices, with_halo(): lax.ppermute(tail, axis, [(i, (i + 1) % count) for i in range(ends)])  11 us
    reduce_sum x6, other arithmetic, restrict(): return jnp.mean(folded, axis=(-4, -2))  10.4 us
    mul x12, other arithmetic, diffuse(): grad_z = face_z * (field_z[:, :, 1:] - field_z[:, :, :-1])  5.71 us
    add x11, other arithmetic, diffuse(): return current + step_size * (flux + source_in)  5.25 us
  transfers between devices with their start and end apart: 31, of which 15 were waited for; matrix products, arithmetic and copies ran while one was open for 10% of the time, Pallas kernels for 0%

commit v1 on v0

v1 whole, which is shorter than its diff:
```python
import functools

import jax
import jax.numpy as jnp
from jax import lax
from jax.experimental import pallas as pl
from jax.experimental.pallas import tpu as pltpu
from jax.sharding import PartitionSpec as P

FSTEPS = 4
CSTEPS = 2
PAD = 8
CHUNK = 64

conductivity_table = (1.0, 0.72, 0.52, 0.37, 0.26, 0.18, 0.13, 0.09)
fine_step = 0.15
coarse_step = 0.3

MESH = pl.DeviceIdType.MESH


def lookup(material):
    result = jnp.zeros(material.shape, jnp.float32)
    for number in range(8):
        result = jnp.where(material == number, jnp.float32(conductivity_table[number]), result)
    return result


def kernel(slabs, blocks, starts, material, source, out, ub, kb, wx, wyl, wyh, wzl, wzh, c0, hs, arrived,
           ru_pad, rf_pad, kc_pad, sc_pad, kcw, cw, gu, gu2, rb, rf, send_e, ec, tmp,
           load_sem, fs, fr, ks, kr, cs, cr, gs, gr, hs_sem, hr_sem, us, ur, vs, vr, es, er, bs, br):
    nx, ny, nz = out.shape
    ncx, ncy = nx // 2, ny // 2
    rows = ncy // slabs
    side = (kc_pad.shape[1] - ncy) // 2
    width = rows + 2 * side
    tm = lax.axis_index("tm")
    sp = lax.axis_index("space")
    has_low = sp > 0
    has_high = sp < blocks - 1
    pending = []

    def remote(cond, src, dst, send, recv, **where):
        copy = pltpu.make_async_remote_copy(
            src_ref=src, dst_ref=dst, send_sem=send, recv_sem=recv, device_id=where, device_id_type=MESH
        )

        @pl.when(cond)
        def _():
            copy.start()

        pending.append((cond, copy))

    def arrive(cond, dst, recv):
        copy = pltpu.make_async_remote_copy(
            src_ref=dst, dst_ref=dst, send_sem=recv, recv_sem=recv, device_id={"tm": tm}, device_id_type=MESH
        )

        @pl.when(cond)
        def _():
            copy.wait_recv()

    def halo(low_src, low_dst, high_src, high_dst, send, recv):
        remote(has_low, low_src, low_dst, send.at[0], recv.at[0], space=sp - 1)
        remote(has_high, high_src, high_dst, send.at[1], recv.at[1], space=sp + 1)

    def halo_wait(low_dst, high_dst, recv):
        arrive(has_high, low_dst, recv.at[0])
        arrive(has_low, high_dst, recv.at[1])

    barrier = pltpu.get_barrier_semaphore()

    @pl.when(has_low)
    def _():
        pl.semaphore_signal(barrier, inc=1, device_id={"space": sp - 1}, device_id_type=MESH)

    @pl.when(has_high)
    def _():
        pl.semaphore_signal(barrier, inc=1, device_id={"space": sp + 1}, device_id_type=MESH)

    for by in range(1, slabs):
        pl.semaphore_signal(barrier, inc=1, device_id={"tm": lax.rem(tm + by, slabs)}, device_id_type=MESH)

    load = pltpu.make_async_copy(starts.at[0], ub.at[0, pl.ds(1, nx), pl.ds(PAD, ny)], load_sem)
    load.start()

    strip = jnp.zeros((PAD, nz), jnp.float32)

    def clear_rows(plane, carry):
        for step in range(FSTEPS):
            ub[step, plane, 0:PAD] = strip
            ub[step, plane, PAD + ny:PAD + ny + PAD] = strip
        kb[plane, 0:PAD] = strip
        kb[plane, PAD + ny:PAD + ny + PAD] = strip
        return carry

    lax.fori_loop(1, nx + 1, clear_rows, 0)
    for ref in (ru_pad, rf_pad, kc_pad, sc_pad):
        for plane in range(ncx):
            ref[plane, 0:side] = jnp.zeros((side, nz), jnp.float32)
            ref[plane, side + ncy:side + ncy + side] = jnp.zeros((side, nz), jnp.float32)

    def clear_ghosts(fine, coarse):
        for step in range(FSTEPS):
            ub[step, fine, PAD:PAD + ny] = jnp.zeros((ny, nz), jnp.float32)
        kb[fine, PAD:PAD + ny] = jnp.zeros((ny, nz), jnp.float32)
        blank = jnp.zeros((width, nz), jnp.float32)
        kcw[coarse] = blank
        for step in range(CSTEPS):
            for slab in range(slabs - 1):
                gu[step, slab, coarse] = blank
                rb[step, slab, coarse] = blank

    @pl.when(jnp.logical_not(has_low))
    def _():
        clear_ghosts(0, 0)

    @pl.when(jnp.logical_not(has_high))
    def _():
        clear_ghosts(nx + 1, ncx + 1)

    def conduct(plane):
        for at in range(0, ny, CHUNK):
            kb[plane + 1, PAD + at:PAD + at + CHUNK] = lookup(material[plane, at:at + CHUNK])

    conduct(0)
    conduct(nx - 1)

    pl.semaphore_wait(barrier, slabs - 1 + has_low.astype(jnp.int32) + has_high.astype(jnp.int32))

    inner = pl.ds(PAD, ny)
    halo(kb.at[1, inner], kb.at[nx + 1, inner], kb.at[nx, inner], kb.at[0, inner], ks, kr)
    load.wait()

    def send_fine(step):
        halo(ub.at[step, 1, inner], ub.at[step, nx + 1, inner], ub.at[step, nx, inner], ub.at[step, 0, inner],
             fs.at[step], fr.at[step])

    def wait_fine(step):
        halo_wait(ub.at[step, nx + 1, inner], ub.at[step, 0, inner], fr.at[step])

    send_fine(0)

    def restrict_plane(pick, plane, base):
        total = pick(2 * plane, base) + pick(2 * plane, base + 1)
        return (total + pick(2 * plane + 1, base) + pick(2 * plane + 1, base + 1)) * 0.25

    def restrict_into(pad_ref, pick, base, scale=1.0):
        for plane in range(ncx):
            value = restrict_plane(pick, plane, base)
            pad_ref[plane, side:side + ncy] = value * scale if scale != 1.0 else value

    restrict_into(ru_pad, lambda plane, at: ub[0, plane + 1, pl.ds(at, ncy, stride=2)], PAD)

    def strip_of(ref, number):
        return ref.at[:, pl.ds(rows * number, width)]

    for to in range(slabs):
        remote(jnp.logical_and(tm != to, tm > 0), strip_of(ru_pad, to),
               gu.at[0, jnp.maximum(tm - 1, 0), pl.ds(1, ncx)], us.at[to], ur.at[tm], tm=to)

    def conduct_loop(plane, carry):
        conduct(plane)
        return carry

    lax.fori_loop(1, nx - 1, conduct_loop, 0)
    restrict_into(kc_pad, lambda plane, at: kb[plane + 1, pl.ds(at, ncy, stride=2)], PAD)
    restrict_into(sc_pad, lambda plane, at: source[plane, pl.ds(at, ncy, stride=2)], 0, coarse_step)
    mine = pl.ds(pl.multiple_of(rows * tm, 8), width)
    for plane in range(ncx):
        kcw[plane + 1] = kc_pad[plane, mine]
    halo(kcw.at[1], kcw.at[ncx + 1], kcw.at[ncx], kcw.at[0], cs, cr)

    def fine_weights(plane):
        half = 0.5 * fine_step
        for at in range(0, ny, CHUNK):
            r = slice(PAD + at, PAD + at + CHUNK)
            q = slice(at, at + CHUNK)
            k = kb[plane + 1, r]
            lane = lax.broadcasted_iota(jnp.int32, k.shape, 1)
            x_low = half * (k + kb[plane, r])
            x_high = half * (k + kb[plane + 2, r])
            y_low = half * (k + kb[plane + 1, PAD + at - 1:PAD + at - 1 + CHUNK])
            y_high = half * (k + kb[plane + 1, PAD + at + 1:PAD + at + 1 + CHUNK])
            first, last = lane == 0, lane == nz - 1
            z_low = half * (k + jnp.where(first, 0.0, pltpu.roll(k, 1, 1)))
            z_high = half * (k + jnp.where(last, 0.0, pltpu.roll(k, nz - 1, 1)))
            wx[plane, q] = x_low
            wx[plane + 1, q] = x_high
            wyl[plane, q] = y_low
            wyh[plane, q] = y_high
            wzl[plane, q] = jnp.where(first, 0.0, z_low)
            wzh[plane, q] = jnp.where(last, 0.0, z_high)
            c0[plane, q] = 1.0 - (x_low + x_high + y_low + y_high + z_low + z_high)
            hs[plane, q] = fine_step * source[plane, q]

    def weights_loop(plane, carry):
        fine_weights(plane)
        return carry

    lax.fori_loop(1, nx - 1, weights_loop, 0)
    halo_wait(kb.at[nx + 1, inner], kb.at[0, inner], kr)
    fine_weights(0)
    fine_weights(nx - 1)

    def fine_plane(step, plane):
        for at in range(0, ny, CHUNK):
            r = slice(PAD + at, PAD + at + CHUNK)
            q = slice(at, at + CHUNK)
            u = ub[step, plane + 1, r]
            total = c0[plane, q] * u + hs[plane, q]
            total += wx[plane, q] * ub[step, plane, r]
            total += wx[plane + 1, q] * ub[step, plane + 2, r]
            total += wyl[plane, q] * ub[step, plane + 1, PAD + at - 1:PAD + at - 1 + CHUNK]
            total += wyh[plane, q] * ub[step, plane + 1, PAD + at + 1:PAD + at + 1 + CHUNK]
            total += wzl[plane, q] * pltpu.roll(u, 1, 1)
            total += wzh[plane, q] * pltpu.roll(u, nz - 1, 1)
            ub[step + 1, plane + 1, r] = total

    def coarse_weights():
        halo_wait(kcw.at[ncx + 1], kcw.at[0], cr)
        half = 0.5 * coarse_step
        near = 0.25 * half
        shape = (width, nz)
        lane = lax.broadcasted_iota(jnp.int32, shape, 1)
        row = lax.broadcasted_iota(jnp.int32, shape, 0) + (rows * tm - side)
        first, last = lane == 0, lane == nz - 1
        low_in = jnp.logical_and(row >= 1, row < ncy)
        high_in = jnp.logical_and(row >= 0, row < ncy - 1)
        for plane in range(ncx):
            k = kcw[plane + 1]
            x_low = near * (k + kcw[plane])
            x_high = near * (k + kcw[plane + 2])
            y_low = near * (k + pltpu.roll(k, 1, 0))
            y_high = near * (k + pltpu.roll(k, width - 1, 0))
            z_low = half * (k + jnp.where(first, 0.0, pltpu.roll(k, 1, 1)))
            z_high = half * (k + jnp.where(last, 0.0, pltpu.roll(k, nz - 1, 1)))
            cw[0, plane] = 1.0 - (x_low + x_high + y_low + y_high + z_low + z_high)
            cw[1, plane] = x_low
            cw[2, plane] = x_high
            cw[3, plane] = jnp.where(low_in, y_low, 0.0)
            cw[4, plane] = jnp.where(high_in, y_high, 0.0)
            cw[5, plane] = jnp.where(first, 0.0, z_low)
            cw[6, plane] = jnp.where(last, 0.0, z_high)
            cw[7, plane] = sc_pad[plane, mine]

    def coarse_plane(ref, step, slab, plane):
        v = ref[step, slab, plane + 1]
        total = cw[0, plane] * v + cw[7, plane]
        total += cw[1, plane] * ref[step, slab, plane]
        total += cw[2, plane] * ref[step, slab, plane + 2]
        total += cw[3, plane] * pltpu.roll(v, 1, 0)
        total += cw[4, plane] * pltpu.roll(v, width - 1, 0)
        total += cw[5, plane] * pltpu.roll(v, 1, 1)
        total += cw[6, plane] * pltpu.roll(v, nz - 1, 1)
        return total

    def send_start(step):
        halo(gu.at[step, :, 1], gu.at[step, :, ncx + 1], gu.at[step, :, ncx], gu.at[step, :, 0],
             gs.at[step], gr.at[step])

    def wait_start(step):
        halo_wait(gu.at[step, :, ncx + 1], gu.at[step, :, 0], gr.at[step])

    def coarse_starts(stage):
        if stage == 0:
            for slab in range(1, slabs):
                arrive(tm != slab, gu.at[0, slab - 1, pl.ds(1, ncx)], ur.at[slab])

                @pl.when(tm == slab)
                def _():
                    for plane in range(ncx):
                        gu[0, slab - 1, plane + 1] = ru_pad[plane, mine]

            send_start(0)
            coarse_weights()
        elif stage == 1:
            wait_start(0)
            for slab in range(slabs - 1):
                for plane in range(ncx):
                    gu[1, slab, plane + 1] = coarse_plane(gu, 0, slab, plane)
            send_start(1)
        elif stage == 2:
            wait_start(1)
            for slab in range(slabs - 1):
                for plane in range(ncx):
                    gu2[slab, plane] = coarse_plane(gu, 1, slab, plane)

    for step in range(FSTEPS):
        wait_fine(step)
        fine_plane(step, 0)
        fine_plane(step, nx - 1)
        if step < FSTEPS - 1:
            send_fine(step + 1)

        def fine_loop(plane, carry, step=step):
            fine_plane(step, plane)
            return carry

        lax.fori_loop(1, nx - 1, fine_loop, 0)
        coarse_starts(step)

    restrict_into(rf_pad, lambda plane, at: ub[FSTEPS, plane + 1, pl.ds(at, ncy, stride=2)], PAD)
    for to in range(slabs):
        remote(jnp.logical_and(tm != to, tm < slabs - 1), strip_of(rf_pad, to),
               rf.at[jnp.minimum(tm, slabs - 2)], vs.at[to], vr.at[tm], tm=to)
    for pair in range(ncx):
        remote(True, ub.at[FSTEPS, pl.ds(2 * pair + 1, 2), inner], arrived.at[pl.ds(2 * pair, 2)],
               bs.at[pair], br.at[pair], tm=lax.rem(tm + 1, slabs))

    def end_state(slab):
        arrive(tm != slab, rf.at[slab], vr.at[slab])

        @pl.when(tm == slab)
        def _():
            for plane in range(ncx):
                rf[slab, plane] = rf_pad[plane, mine]

    end_state(0)
    for plane in range(ncx):
        rb[0, 0, plane + 1] = rf[0, plane]
    for slab in range(1, slabs):
        at = slab - 1
        for step in range(CSTEPS):
            number = at * CSTEPS + step
            halo(rb.at[step, at, 1], rb.at[step, at, ncx + 1], rb.at[step, at, ncx], rb.at[step, at, 0],
                 hs_sem.at[number], hr_sem.at[number])
            if step == 0 and slab < slabs - 1:
                end_state(slab)
            halo_wait(rb.at[step, at, ncx + 1], rb.at[step, at, 0], hr_sem.at[number])
            for plane in range(ncx):
                value = coarse_plane(rb, step, at, plane)
                if step < CSTEPS - 1:
                    rb[step + 1, at, plane + 1] = value
                else:
                    value = value - gu2[at, plane]
                    send_e[at, plane] = value
                    if slab < slabs - 1:
                        rb[0, at + 1, plane + 1] = value + rf[slab, plane]
        to = (slab + 1) % slabs
        keep = pl.ds(side, rows)
        remote(tm != to, send_e.at[at, :, keep], ec.at[:, pl.ds(pl.multiple_of(rows * tm, 8), rows)],
               es.at[at], er.at[tm], tm=to)

        @pl.when(tm == to)
        def _():
            for plane in range(ncx):
                ec[plane, pl.ds(pl.multiple_of(rows * tm, 8), rows)] = send_e[at, plane, side:side + rows]

    @pl.when(tm == 1)
    def _():
        for plane in range(ncx):
            ec[plane] = jnp.zeros((ncy, nz), jnp.float32)

    for by in range(slabs):
        arrive(jnp.logical_and(tm != 1, tm != by), ec.at[:, pl.ds(rows * by, rows)], er.at[by])
    for plane in range(ncx):
        value = ec[plane]
        tmp[plane, pl.ds(0, ncy, stride=2)] = value
        tmp[plane, pl.ds(1, ncy, stride=2)] = value
    for pair in range(ncx):
        arrive(True, arrived.at[pl.ds(2 * pair, 2)], br.at[pair])
        for at in range(0, ny, CHUNK):
            q = slice(at, at + CHUNK)
            out[2 * pair, q] = arrived[2 * pair, q] + tmp[pair, q]
            out[2 * pair + 1, q] = arrived[2 * pair + 1, q] + tmp[pair, q]
    for cond, copy in pending:
        @pl.when(cond)
        def _(copy=copy):
            copy.wait_send()


def local(starts, material, source):
    slabs = lax.axis_size("tm")
    blocks = lax.axis_size("space")
    nx, ny, nz = source.shape
    ncx, ncy = nx // 2, ny // 2
    side = -(-CSTEPS * (slabs - 1) // 8) * 8
    width = ncy // slabs + 2 * side
    f32 = functools.partial(pltpu.VMEM, dtype=jnp.float32)
    sems = lambda *shape: pltpu.SemaphoreType.DMA(shape)
    field = (nx, ny, nz)
    padded = (ncx, ncy + 2 * side, nz)
    live = slabs - 1
    scratch = [
        f32((FSTEPS + 1, nx + 2, ny + 2 * PAD, nz)),
        f32((nx + 2, ny + 2 * PAD, nz)),
        f32((nx + 1, ny, nz)),
        *[f32(field) for _ in range(7)],
        *[f32(padded) for _ in range(4)],
        f32((ncx + 2, width, nz)),
        f32((8, ncx, width, nz)),
        f32((CSTEPS, live, ncx + 2, width, nz)),
        f32((live, ncx, width, nz)),
        f32((CSTEPS, live, ncx + 2, width, nz)),
        f32((live, ncx, width, nz)),
        f32((live, ncx, width, nz)),
        f32((ncx, ncy, nz)),
        f32((ncx, ny, nz)),
        pltpu.SemaphoreType.DMA,
        sems(FSTEPS, 2), sems(FSTEPS, 2),
        sems(2), sems(2),
        sems(2), sems(2),
        sems(CSTEPS, 2), sems(CSTEPS, 2),
        sems(live * CSTEPS, 2), sems(live * CSTEPS, 2),
        sems(slabs), sems(slabs),
        sems(slabs), sems(slabs),
        sems(slabs), sems(slabs),
        sems(ncx), sems(ncx),
    ]
    vmem = pl.BlockSpec(memory_space=pltpu.VMEM)
    result = pl.pallas_call(
        functools.partial(kernel, slabs, blocks),
        out_shape=jax.ShapeDtypeStruct(field, jnp.float32),
        in_specs=[pl.BlockSpec(memory_space=pl.ANY), vmem, vmem],
        out_specs=vmem,
        scratch_shapes=scratch,
        compiler_params=pltpu.CompilerParams(
            collective_id=0, has_side_effects=True, vmem_limit_bytes=48 * 1024 * 1024
        ),
    )(starts, material, source)
    return result[None]


def solution(mesh):
    in_specs = (P("tm", "space", None, None), P("space", None, None), P("space", None, None))
    out_specs = P("tm", "space", None, None)
    return jax.shard_map(local, mesh=mesh, in_specs=in_specs, out_specs=out_specs, check_vma=False)
```

time: 222 us -> 63.4 us (0.29)
  starting transfers between devices: 97 us -> 0 us
  waiting for transfers between devices: 67.6 us -> 0 us
  Pallas kernels: 0 us -> 58.5 us
  other arithmetic: 42.7 us -> 0 us
  local copies, waits for them, and re-layouts: 12.7 us -> 4.65 us
    ppermute x31 -> x0, starting transfers between devices: 97 us -> none  [the longest x13 53.8 us: with_halo(): lax.ppermute(tail, axis, [(i, (i + 1) % count) for i in range(ends)])]
    ppermute x31 -> x0, waiting for transfers between devices: 67.6 us -> none  [the longest x5 55.7 us: shifted(): return lax.ppermute(x, axis, pairs)]
    pallas_call x0 -> x1, Pallas kernels: none -> 58.5 us  [local(): pl.pallas_call(functools.partial(kernel, slabs, blocks), out_shape=jax.Sh...]
    mul x36 -> x0, other arithmetic: 12.8 us -> none  [the longest x12 5.71 us: diffuse(): grad_z = face_z * (field_z[:, :, 1:] - field_z[:, :, :-1])]
    reduce_sum x6 -> x0, other arithmetic: 10.4 us -> none  [restrict(): return jnp.mean(folded, axis=(-4, -2))]
    add x12 -> x0, other arithmetic: 6.68 us -> none  [the longest x11 5.25 us: diffuse(): return current + step_size * (flux + source_in)]
    slice x18 -> x0, local copies, waits for them, and re-layouts: 5.44 us -> none  [the longest x12 2.36 us: with_halo(): lax.slice_in_dim(cells, cells.shape[dim] - width, cells.shape[dim], axis=...]
    broadcast_in_dim x5 -> x0, local copies, waits for them, and re-layouts: 4.2 us -> none  [prolong(): jnp.broadcast_to(values[..., :, None, :, None, :], lead_dims + (rows_x, 2...]
  transfers between devices with their start and end apart: 31 -> 0, of which waited for: 15 -> 0; matrix products, arithmetic and copies ran while one was open for 10% -> 0% of each run, Pallas kernels for 0% -> 0%
where the time goes in v1:
time: 63.4 us; the launch traced here: 63.2 us
  Pallas kernels  58.5 us (92%)
  local copies, waits for them, and re-layouts  4.65 us (7%)
    pallas_call x1, Pallas kernels, local(): pl.pallas_call(functools.partial(kernel, slabs, blocks), out_shape=jax.Sh...  58.5 us
    unnamed x7, local copies, waits for them, and re-layouts  4.65 us

profile of v1, /device:TPU:1, one launch (start us, length us, event | category | flops | bytes accessed | tf_op | source)
XLA Modules:
  0.0 63.2 jit_solution(12136079368532287914)
XLA Ops:
  0.0 0.0 copy-start
  0.0 1.2 %copy-done = f32[1,8,256,128]{3,2,1,0:T(8,128)S(1)} copy-done((f32[1,8,256,128]{3,2,1,0:T(8,128)S(1)}, f32[1,8,256,128]{3,2,1,0:T(8,128)}, u32[]{:S(2)}) %copy-start) | copy-done | bytes 1048600
  1.2 0.0 copy-start.1
  1.2 1.2 %copy-done.1 = s32[8,256,128]{2,1,0:T(8,128)S(1)} copy-done((s32[8,256,128]{2,1,0:T(8,128)S(1)}, s32[8,256,128]{2,1,0:T(8,128)}, u32[]{:S(2)}) %copy-start.1) | copy-done | bytes 1048600
  2.5 0.0 copy-start.2
  2.5 1.2 %copy-done.2 = f32[8,256,128]{2,1,0:T(8,128)S(1)} copy-done((f32[8,256,128]{2,1,0:T(8,128)S(1)}, f32[8,256,128]{2,1,0:T(8,128)}, u32[]{:S(2)}) %copy-start.2) | copy-done | bytes 1048600
  3.7 58.5 %shard_map.37 = f32[8,256,128]{2,1,0:T(8,128)S(1)} custom-call(f32[1,8,256,128]{3,2,1,0:T(8,128)S(1)} %copy-done, s32[8,256,128]{2,1,0:T(8,128)S(1)} %copy-done.1, f32[8,256,128]{2,1,0:T(8,128)S(1)} %copy-done.2), custom_call_target="tpu_custom_call" | custom-call | tf_op jit(solution)/shard_map/pallas_call | solution.py:412
  62.2 1.0 %copy.5 = f32[1,8,256,128]{3,2,1,0:T(8,128)} copy(f32[1,8,256,128]{3,2,1,0:T(8,128)S(1)} %bitcast.1) | data formatting | bytes 2097152
Async XLA Ops:
  0.0 1.2 %copy-start = (f32[1,8,256,128]{3,2,1,0:T(8,128)S(1)}, f32[1,8,256,128]{3,2,1,0:T(8,128)}, u32[]{:S(2)}) copy-start(f32[1,8,256,128]{3,2,1,0:T(8,128)} %starts.1) | copy-start | bytes 3145732
  1.2 1.2 %copy-start.1 = (s32[8,256,128]{2,1,0:T(8,128)S(1)}, s32[8,256,128]{2,1,0:T(8,128)}, u32[]{:S(2)}) copy-start(s32[8,256,128]{2,1,0:T(8,128)} %material.1) | copy-start | bytes 3145732
  2.5 1.2 %copy-start.2 = (f32[8,256,128]{2,1,0:T(8,128)S(1)}, f32[8,256,128]{2,1,0:T(8,128)}, u32[]{:S(2)}) copy-start(f32[8,256,128]{2,1,0:T(8,128)} %source.1) | copy-start | bytes 3145732

commit v2 on v1

v2 whole, which is shorter than its diff:
```python
import functools

import jax
import jax.numpy as jnp
from jax import lax
from jax.experimental import pallas as pl
from jax.experimental.pallas import tpu as pltpu
from jax.sharding import PartitionSpec as P

FSTEPS = 4
CSTEPS = 2
PAD = 8
CHUNK = 64

conductivity_table = (1.0, 0.72, 0.52, 0.37, 0.26, 0.18, 0.13, 0.09)
fine_step = 0.15
coarse_step = 0.3

MESH = pl.DeviceIdType.MESH


def lookup(material):
    result = jnp.zeros(material.shape, jnp.float32)
    for number in range(8):
        result = jnp.where(material == number, jnp.float32(conductivity_table[number]), result)
    return result


def kernel(slabs, blocks, starts, material, source, out, mat, src, ub, ub2, kb, wx, wyl, wyh, wzl, wzh, c0, hs, full,
           kcb, cw, rub, rum, delta, rb, rm, got, last_state, ec, tmp, load_sem,
           fs, fr, f2s, f2r, ks, kr, cs, cr, chs, chr_, us, ur, vs, vr, es, er, bs, br):
    nx, ny, nz = src.shape
    ncx, ncy = nx // 2, ny // 2
    early = ub2.shape[2] - 2 * PAD
    whole = kcb.shape[1]
    side = (whole - ncy) // 2
    rows = ncy // slabs
    width = rows + 2 * side
    late = early - 8
    live = slabs - 1
    tm = lax.axis_index("tm")
    sp = lax.axis_index("space")
    has_low = sp > 0
    has_high = sp < blocks - 1
    after = lax.rem(tm + 1, slabs)
    pending = []

    def remote(cond, src_ref, dst_ref, send, recv, **where):
        copy = pltpu.make_async_remote_copy(
            src_ref=src_ref, dst_ref=dst_ref, send_sem=send, recv_sem=recv, device_id=where, device_id_type=MESH
        )

        @pl.when(cond)
        def _():
            copy.start()

        pending.append((cond, copy))

    def arrive(cond, dst_ref, recv):
        copy = pltpu.make_async_remote_copy(
            src_ref=dst_ref, dst_ref=dst_ref, send_sem=recv, recv_sem=recv, device_id={"tm": tm}, device_id_type=MESH
        )

        @pl.when(cond)
        def _():
            copy.wait_recv()

    def halo(low_src, low_dst, high_src, high_dst, send, recv):
        remote(has_low, low_src, low_dst, send.at[0], recv.at[0], space=sp - 1)
        remote(has_high, high_src, high_dst, send.at[1], recv.at[1], space=sp + 1)

    def halo_wait(low_dst, high_dst, recv):
        arrive(has_high, low_dst, recv.at[0])
        arrive(has_low, high_dst, recv.at[1])

    barrier = pltpu.get_barrier_semaphore()

    @pl.when(has_low)
    def _():
        pl.semaphore_signal(barrier, inc=1, device_id={"space": sp - 1}, device_id_type=MESH)

    @pl.when(has_high)
    def _():
        pl.semaphore_signal(barrier, inc=1, device_id={"space": sp + 1}, device_id_type=MESH)

    for by in range(1, slabs):
        pl.semaphore_signal(barrier, inc=1, device_id={"tm": lax.rem(tm + by, slabs)}, device_id_type=MESH)

    load_mat = pltpu.make_async_copy(material, mat, load_sem.at[0])
    load_mat.start()
    load_u = pltpu.make_async_copy(starts.at[0], ub.at[0, pl.ds(1, nx), pl.ds(PAD, ny)], load_sem.at[1])
    load_u.start()
    load_src = pltpu.make_async_copy(source, src, load_sem.at[2])
    load_src.start()

    strip = jnp.zeros((PAD, nz), jnp.float32)

    def clear_rows(plane, carry):
        for step in range(FSTEPS):
            ub[step, plane, 0:PAD] = strip
            ub[step, plane, PAD + ny:PAD + ny + PAD] = strip
            ub2[step, plane, 0:PAD] = strip
            ub2[step, plane, PAD + early:PAD + early + PAD] = strip
        kb[plane, 0:PAD] = strip
        kb[plane, PAD + ny:PAD + ny + PAD] = strip
        return carry

    lax.fori_loop(1, nx + 1, clear_rows, 0)
    edge = jnp.zeros((side, nz), jnp.float32)

    def clear_sides(plane, carry):
        for ref in (kcb, rub):
            ref[plane, 0:side] = edge
            ref[plane, side + ncy:whole] = edge
        return carry

    lax.fori_loop(0, ncx + 4, clear_sides, 0)
    for plane in range(ncx + 2):
        cw[7, plane, 0:side] = edge
        cw[7, plane, side + ncy:whole] = edge
    for plane in range(ncx):
        delta[plane, 0:side] = edge
        delta[plane, side + ncy:whole] = edge

    def clear_ghosts(fine, coarse):
        for step in range(FSTEPS):
            ub[step, fine, PAD:PAD + ny] = jnp.zeros((ny, nz), jnp.float32)
            ub2[step, fine, PAD:PAD + early] = jnp.zeros((early, nz), jnp.float32)
        kb[fine, PAD:PAD + ny] = jnp.zeros((ny, nz), jnp.float32)
        for plane in (coarse, coarse + 1):
            kcb[plane] = jnp.zeros((whole, nz), jnp.float32)
            rub[plane] = jnp.zeros((whole, nz), jnp.float32)
            for slab in range(live):
                rb[slab, plane] = jnp.zeros((width, nz), jnp.float32)

    @pl.when(jnp.logical_not(has_low))
    def _():
        clear_ghosts(0, 0)
        cw[7, 0] = jnp.zeros((whole, nz), jnp.float32)

    @pl.when(jnp.logical_not(has_high))
    def _():
        clear_ghosts(nx + 1, ncx + 2)
        cw[7, ncx + 1] = jnp.zeros((whole, nz), jnp.float32)

    def conduct(plane):
        for at in range(0, ny, CHUNK):
            kb[plane + 1, PAD + at:PAD + at + CHUNK] = lookup(mat[plane, at:at + CHUNK])

    load_mat.wait()
    conduct(0)
    conduct(nx - 1)
    pl.semaphore_wait(barrier, slabs - 1 + has_low.astype(jnp.int32) + has_high.astype(jnp.int32))

    inner = pl.ds(PAD, ny)
    first_rows = pl.ds(PAD, early)
    halo(starts.at[0, 0], ub.at[0, nx + 1, inner], starts.at[0, nx - 1], ub.at[0, 0, inner], fs.at[0], fr.at[0])
    halo(kb.at[1, inner], kb.at[nx + 1, inner], kb.at[nx, inner], kb.at[0, inner], ks, kr)
    for pair in range(ncx):
        remote(True, starts.at[0, pl.ds(2 * pair, 2), pl.ds(0, early)],
               ub2.at[0, pl.ds(2 * pair + 1, 2), first_rows], us.at[pair], ur.at[pair], tm=after)

    def send_fine(step):
        halo(ub.at[step, 1, inner], ub.at[step, nx + 1, inner], ub.at[step, nx, inner], ub.at[step, 0, inner],
             fs.at[step], fr.at[step])

    def wait_fine(step):
        halo_wait(ub.at[step, nx + 1, inner], ub.at[step, 0, inner], fr.at[step])

    def send_early(step):
        halo(ub2.at[step, 1, first_rows], ub2.at[step, nx + 1, first_rows],
             ub2.at[step, nx, first_rows], ub2.at[step, 0, first_rows], f2s.at[step], f2r.at[step])

    def wait_early(step):
        halo_wait(ub2.at[step, nx + 1, first_rows], ub2.at[step, 0, first_rows], f2r.at[step])

    def conduct_loop(plane, carry):
        conduct(plane)
        return carry

    lax.fori_loop(1, nx - 1, conduct_loop, 0)

    load_src.wait()

    def fine_weights(plane):
        half = 0.5 * fine_step
        for at in range(0, ny, CHUNK):
            r = slice(PAD + at, PAD + at + CHUNK)
            q = slice(at, at + CHUNK)
            k = kb[plane + 1, r]
            lane = lax.broadcasted_iota(jnp.int32, k.shape, 1)
            x_low = half * (k + kb[plane, r])
            x_high = half * (k + kb[plane + 2, r])
            y_low = half * (k + kb[plane + 1, PAD + at - 1:PAD + at - 1 + CHUNK])
            y_high = half * (k + kb[plane + 1, PAD + at + 1:PAD + at + 1 + CHUNK])
            first, last = lane == 0, lane == nz - 1
            z_low = half * (k + jnp.where(first, 0.0, pltpu.roll(k, 1, 1)))
            z_high = half * (k + jnp.where(last, 0.0, pltpu.roll(k, nz - 1, 1)))
            wx[plane, q] = x_low
            wx[plane + 1, q] = x_high
            wyl[plane, q] = y_low
            wyh[plane, q] = y_high
            wzl[plane, q] = jnp.where(first, 0.0, z_low)
            wzh[plane, q] = jnp.where(last, 0.0, z_high)
            c0[plane, q] = 1.0 - (x_low + x_high + y_low + y_high + z_low + z_high)
            hs[plane, q] = fine_step * src[plane, q]

    def weights_loop(plane, carry):
        fine_weights(plane)
        return carry

    lax.fori_loop(1, nx - 1, weights_loop, 0)
    halo_wait(kb.at[nx + 1, inner], kb.at[0, inner], kr)
    fine_weights(0)
    fine_weights(nx - 1)
    load_u.wait()

    def fine_plane(ref, plane, count, store):
        for at in range(0, count, CHUNK):
            size = min(CHUNK, count - at)
            q = slice(at, at + size)
            r = slice(PAD + at, PAD + at + size)
            u = ref[plane + 1, r]
            total = c0[plane, q] * u + hs[plane, q]
            total += wx[plane, q] * ref[plane, r]
            total += wx[plane + 1, q] * ref[plane + 2, r]
            total += wyl[plane, q] * ref[plane + 1, PAD + at - 1:PAD + at - 1 + size]
            total += wyh[plane, q] * ref[plane + 1, PAD + at + 1:PAD + at + 1 + size]
            total += wzl[plane, q] * pltpu.roll(u, 1, 1)
            total += wzh[plane, q] * pltpu.roll(u, nz - 1, 1)
            store(plane, at, size, total)

    def sweep(ref, count, store, send):
        fine_plane(ref, 0, count, store)
        fine_plane(ref, nx - 1, count, store)
        send()

        def fine_loop(plane, carry):
            fine_plane(ref, plane, count, store)
            return carry

        lax.fori_loop(1, nx - 1, fine_loop, 0)

    def into(ref):
        def store(plane, at, size, value):
            ref[plane + 1, PAD + at:PAD + at + size] = value
        return store

    def restrict_plane(ref, plane, base):
        total = ref[plane, pl.ds(base, ncy, stride=2)] + ref[plane, pl.ds(base + 1, ncy, stride=2)]
        total += ref[plane + 1, pl.ds(base, ncy, stride=2)]
        total += ref[plane + 1, pl.ds(base + 1, ncy, stride=2)]
        return total * 0.25

    core = slice(side, side + ncy)
    mid = pl.ds(side, ncy)

    def coarse_inputs():
        for plane in range(ncx):
            rub[plane + 2, core] = restrict_plane(ub.at[0], 2 * plane + 1, PAD)
            kcb[plane + 2, core] = restrict_plane(kb, 2 * plane + 1, PAD)
            cw[7, plane + 1, core] = coarse_step * restrict_plane(src, 2 * plane, 0)
        low, high = pl.ds(2, 2), pl.ds(ncx, 2)
        low_ghost, high_ghost = pl.ds(0, 2), pl.ds(ncx + 2, 2)
        halo(kcb.at[low, mid], kcb.at[high_ghost, mid], kcb.at[high, mid], kcb.at[low_ghost, mid], cs.at[0], cr.at[0])
        halo(rub.at[low, mid], rub.at[high_ghost, mid], rub.at[high, mid], rub.at[low_ghost, mid], cs.at[1], cr.at[1])
        halo(cw.at[7, 1, mid], cw.at[7, ncx + 1, mid], cw.at[7, ncx, mid], cw.at[7, 0, mid], cs.at[2], cr.at[2])

    def coarse_weights():
        low_ghost, high_ghost = pl.ds(0, 2), pl.ds(ncx + 2, 2)
        halo_wait(kcb.at[high_ghost, mid], kcb.at[low_ghost, mid], cr.at[0])
        halo_wait(rub.at[high_ghost, mid], rub.at[low_ghost, mid], cr.at[1])
        halo_wait(cw.at[7, ncx + 1, mid], cw.at[7, 0, mid], cr.at[2])
        half = 0.5 * coarse_step
        near = 0.25 * half
        shape = (whole, nz)
        lane = lax.broadcasted_iota(jnp.int32, shape, 1)
        row = lax.broadcasted_iota(jnp.int32, shape, 0) - side
        first, last = lane == 0, lane == nz - 1
        low_in = jnp.logical_and(row >= 1, row < ncy)
        high_in = jnp.logical_and(row >= 0, row < ncy - 1)
        for plane in range(ncx + 2):
            k = kcb[plane + 1]
            x_low = near * (k + kcb[plane])
            x_high = near * (k + kcb[plane + 2])
            y_low = near * (k + pltpu.roll(k, 1, 0))
            y_high = near * (k + pltpu.roll(k, whole - 1, 0))
            z_low = half * (k + jnp.where(first, 0.0, pltpu.roll(k, 1, 1)))
            z_high = half * (k + jnp.where(last, 0.0, pltpu.roll(k, nz - 1, 1)))
            cw[0, plane] = 1.0 - (x_low + x_high + y_low + y_high + z_low + z_high)
            cw[1, plane] = jnp.where(has_high, x_low, 0.0) if plane == ncx + 1 else x_low
            cw[2, plane] = jnp.where(has_low, x_high, 0.0) if plane == 0 else x_high
            cw[3, plane] = jnp.where(low_in, y_low, 0.0)
            cw[4, plane] = jnp.where(high_in, y_high, 0.0)
            cw[5, plane] = jnp.where(first, 0.0, z_low)
            cw[6, plane] = jnp.where(last, 0.0, z_high)

    def coarse_plane(ref, plane, pick, offset):
        v = ref[plane + 1]
        at = plane + offset
        total = cw[0, at, pick] * v + cw[7, at, pick]
        total += cw[1, at, pick] * ref[plane]
        total += cw[2, at, pick] * ref[plane + 2]
        total += cw[3, at, pick] * pltpu.roll(v, 1, 0)
        total += cw[4, at, pick] * pltpu.roll(v, v.shape[0] - 1, 0)
        total += cw[5, at, pick] * pltpu.roll(v, 1, 1)
        total += cw[6, at, pick] * pltpu.roll(v, nz - 1, 1)
        return total

    def coarse_map(ref, middle, pick, store):
        for plane in range(ncx + 2):
            middle[plane] = coarse_plane(ref, plane, pick, 0)
        for plane in range(ncx):
            store(plane, coarse_plane(middle, plane, pick, 1))

    for step in range(FSTEPS):
        wait_fine(step)

        def send(step=step):
            if step < FSTEPS - 1:
                send_fine(step + 1)

        sweep(ub.at[step], ny, into(ub.at[step + 1]), send)
        if step == 0:
            coarse_inputs()
        if step == FSTEPS - 2:
            coarse_weights()

            def keep_minus(plane, value):
                delta[plane] = jnp.where(tm > 0, -value, 0.0)

            coarse_map(rub, rum, slice(0, whole), keep_minus)

    for plane in range(ncx):
        delta[plane, core] = delta[plane, core] + restrict_plane(ub.at[FSTEPS], 2 * plane + 1, PAD)
    for to in range(slabs):
        remote(tm != to, delta.at[:, pl.ds(rows * to, width)], got.at[tm], vs.at[to], vr.at[tm], tm=to)
    for pair in range(ncx):
        remote(True, ub.at[FSTEPS, pl.ds(2 * pair + 1, 2), pl.ds(PAD + late, ny - late)],
               full.at[pl.ds(2 * pair, 2), pl.ds(late, ny - late)], bs.at[pair], br.at[pair], tm=after)

    mine = pl.ds(pl.multiple_of(rows * tm, 8), width)

    def end_state(slab):
        arrive(tm != slab, got.at[slab], vr.at[slab])

        @pl.when(tm == slab)
        def _():
            for plane in range(ncx):
                got[slab, plane] = delta[plane, mine]

    def send_chain(slab):
        halo(rb.at[slab, pl.ds(2, 2)], rb.at[slab, pl.ds(ncx + 2, 2)], rb.at[slab, pl.ds(ncx, 2)],
             rb.at[slab, pl.ds(0, 2)], chs.at[slab], chr_.at[slab])

    own_rows = pl.ds(pl.multiple_of(rows * tm, 8), rows)

    def chain(slab):
        end_state(slab + 1)
        halo_wait(rb.at[slab, pl.ds(ncx + 2, 2)], rb.at[slab, pl.ds(0, 2)], chr_.at[slab])
        to = (slab + 2) % slabs

        if slab + 1 < live:
            def store(plane, value):
                rb[slab + 1, plane + 2] = value + got[slab + 1, plane]

            coarse_map(rb.at[slab], rm, mine, store)
            send_chain(slab + 1)
            result = rb.at[slab + 1, pl.ds(2, ncx)]
        else:
            def store(plane, value):
                last_state[plane] = value + got[slab + 1, plane]

            coarse_map(rb.at[slab], rm, mine, store)
            result = last_state
        remote(tm != to, result.at[:, pl.ds(side, rows)], ec.at[:, own_rows], es.at[slab], er.at[tm], tm=to)

        @pl.when(tm == to)
        def _():
            for plane in range(ncx):
                ec[plane, own_rows] = result[plane, side:side + rows]

    for pair in range(ncx):
        arrive(True, ub2.at[0, pl.ds(2 * pair + 1, 2), first_rows], ur.at[pair])
    send_early(0)

    def early_step(step):
        wait_early(step)
        if step < FSTEPS - 1:
            sweep(ub2.at[step], early, into(ub2.at[step + 1]), lambda: send_early(step + 1))
        else:
            def store(plane, at, size, value):
                full[plane, at:at + size] = value

            sweep(ub2.at[step], late, store, lambda: None)

    early_step(0)
    end_state(0)
    for plane in range(ncx):
        rb[0, plane + 2] = got[0, plane]
    send_chain(0)
    for turn in range(max(FSTEPS - 1, live)):
        if turn + 1 < FSTEPS:
            early_step(turn + 1)
        if turn < live:
            chain(turn)

    @pl.when(tm == 1)
    def _():
        for plane in range(ncx):
            ec[plane] = jnp.zeros((ncy, nz), jnp.float32)

    for by in range(slabs):
        arrive(jnp.logical_and(tm != 1, tm != by), ec.at[:, pl.ds(rows * by, rows)], er.at[by])
    for pair in range(ncx):
        arrive(True, full.at[pl.ds(2 * pair, 2), pl.ds(late, ny - late)], br.at[pair])
        value = ec[pair] - restrict_plane(full, 2 * pair, 0)
        value = jnp.where(tm == 1, 0.0, value)
        tmp[pair, pl.ds(0, ncy, stride=2)] = value
        tmp[pair, pl.ds(1, ncy, stride=2)] = value
        for at in range(0, ny, CHUNK):
            q = slice(at, at + CHUNK)
            out[2 * pair, q] = full[2 * pair, q] + tmp[pair, q]
            out[2 * pair + 1, q] = full[2 * pair + 1, q] + tmp[pair, q]
    for cond, copy in pending:
        @pl.when(cond)
        def _(copy=copy):
            copy.wait_send()


def local(starts, material, source):
    slabs = lax.axis_size("tm")
    blocks = lax.axis_size("space")
    nx, ny, nz = source.shape
    ncx, ncy = nx // 2, ny // 2
    side = -(-CSTEPS * (slabs - 1) // 8) * 8
    whole = ncy + 2 * side
    width = ncy // slabs + 2 * side
    early = ny * 5 // 64 * 8
    f32 = functools.partial(pltpu.VMEM, dtype=jnp.float32)
    sems = lambda *shape: pltpu.SemaphoreType.DMA(shape)
    field = (nx, ny, nz)
    live = slabs - 1
    scratch = [
        pltpu.VMEM(field, jnp.int32),
        f32(field),
        f32((FSTEPS + 1, nx + 2, ny + 2 * PAD, nz)),
        f32((FSTEPS, nx + 2, early + 2 * PAD, nz)),
        f32((nx + 2, ny + 2 * PAD, nz)),
        f32((nx + 1, ny, nz)),
        *[f32(field) for _ in range(7)],
        f32((ncx + 4, whole, nz)),
        f32((8, ncx + 2, whole, nz)),
        f32((ncx + 4, whole, nz)),
        f32((ncx + 2, whole, nz)),
        f32((ncx, whole, nz)),
        f32((live, ncx + 4, width, nz)),
        f32((ncx + 2, width, nz)),
        f32((slabs, ncx, width, nz)),
        f32((ncx, width, nz)),
        f32((ncx, ncy, nz)),
        f32((ncx, ny, nz)),
        sems(3),
        sems(FSTEPS, 2), sems(FSTEPS, 2),
        sems(FSTEPS, 2), sems(FSTEPS, 2),
        sems(2), sems(2),
        sems(3, 2), sems(3, 2),
        sems(live, 2), sems(live, 2),
        sems(ncx), sems(ncx),
        sems(slabs), sems(slabs),
        sems(slabs), sems(slabs),
        sems(ncx), sems(ncx),
    ]
    hbm = pl.BlockSpec(memory_space=pl.ANY)
    result = pl.pallas_call(
        functools.partial(kernel, slabs, blocks),
        out_shape=jax.ShapeDtypeStruct(field, jnp.float32),
        in_specs=[hbm, hbm, hbm],
        out_specs=pl.BlockSpec(memory_space=pltpu.VMEM),
        scratch_shapes=scratch,
        compiler_params=pltpu.CompilerParams(
            collective_id=0, has_side_effects=True, vmem_limit_bytes=60 * 1024 * 1024
        ),
    )(starts, material, source)
    return result[None]


def solution(mesh):
    in_specs = (P("tm", "space", None, None), P("space", None, None), P("space", None, None))
    out_specs = P("tm", "space", None, None)
    return jax.shard_map(local, mesh=mesh, in_specs=in_specs, out_specs=out_specs, check_vma=False)
```

time: 63.4 us -> 52.8 us (0.83)
  Pallas kernels: 58.5 us -> 50 us
  local copies, waits for them, and re-layouts: 4.65 us -> 2.27 us
    pallas_call x1, Pallas kernels: 58.5 us -> 50 us  [local(): pl.pallas_call(functools.partial(kernel, slabs, blocks), out_shape=jax.Sh...]
    unnamed x7 -> x1, local copies, waits for them, and re-layouts: 4.65 us -> 2.27 us
where the time goes in v2:
time: 52.8 us; the launch traced here: 52.3 us
  Pallas kernels  50 us (95%)
  local copies, waits for them, and re-layouts  2.27 us (4%)
    pallas_call x1, Pallas kernels, local(): pl.pallas_call(functools.partial(kernel, slabs, blocks), out_shape=jax.Sh...  50 us
    unnamed x1, local copies, waits for them, and re-layouts  2.27 us

profile of v2, /device:TPU:1, one launch (start us, length us, event | category | flops | bytes accessed | tf_op | source)
XLA Modules:
  0.0 52.3 jit_solution(5154881114265859016)
XLA Ops:
  0.0 50.0 %shard_map.37 = f32[8,256,128]{2,1,0:T(8,128)} custom-call(f32[1,8,256,128]{3,2,1,0:T(8,128)} %starts.1, s32[8,256,128]{2,1,0:T(8,128)} %material.1, f32[8,256,128]{2,1,0:T(8,128)} %source.1), custom_call_target="tpu_custom_call" | custom-call | tf_op jit(solution)/shard_map/pallas_call | solution.py:475
  50.0 2.3 %copy.5 = f32[1,8,256,128]{3,2,1,0:T(8,128)} copy(f32[1,8,256,128]{3,2,1,0:T(8,128)} %bitcast.1) | data formatting | bytes 2097152

commit v3 on v2

--- a/solution.py
+++ b/solution.py
@@ -26,9 +26,9 @@
     return result
 
 
-def kernel(slabs, blocks, starts, material, source, out, mat, src, ub, ub2, kb, wx, wyl, wyh, wzl, wzh, c0, hs, full,
+def kernel(slabs, blocks, starts, material, source, out, lift, mat, src, ub, ub2, kb, wx, wyl, wyh, wzl, wzh, c0, hs, full,
            kcb, cw, rub, rum, delta, rb, rm, got, last_state, ec, tmp, load_sem,
-           fs, fr, f2s, f2r, ks, kr, cs, cr, chs, chr_, us, ur, vs, vr, es, er, bs, br):
+           fs, fr, f2s, f2r, ks, kr, cs, cr, chs, chr_, us, ur, vs, vr, es, er, bs, br, put_sem):
     nx, ny, nz = src.shape
     ncx, ncy = nx // 2, ny // 2
     early = ub2.shape[2] - 2 * PAD
@@ -179,8 +179,30 @@
         return carry
 
     lax.fori_loop(1, nx - 1, conduct_loop, 0)
-
     load_src.wait()
+    load_u.wait()
+
+    def restrict_plane(ref, plane, base):
+        total = ref[plane, pl.ds(base, ncy, stride=2)] + ref[plane, pl.ds(base + 1, ncy, stride=2)]
+        total += ref[plane + 1, pl.ds(base, ncy, stride=2)]
+        total += ref[plane + 1, pl.ds(base + 1, ncy, stride=2)]
+        return total * 0.25
+
+    core = slice(side, side + ncy)
+    mid = pl.ds(side, ncy)
+
+    def coarse_inputs():
+        for plane in range(ncx):
+            rub[plane + 2, core] = restrict_plane(ub.at[0], 2 * plane + 1, PAD)
+            kcb[plane + 2, core] = restrict_plane(kb, 2 * plane + 1, PAD)
+            cw[7, plane + 1, core] = coarse_step * restrict_plane(src, 2 * plane, 0)
+        low, high = pl.ds(2, 2), pl.ds(ncx, 2)
+        low_ghost, high_ghost = pl.ds(0, 2), pl.ds(ncx + 2, 2)
+        halo(kcb.at[low, mid], kcb.at[high_ghost, mid], kcb.at[high, mid], kcb.at[low_ghost, mid], cs.at[0], cr.at[0])
+        halo(rub.at[low, mid], rub.at[high_ghost, mid], rub.at[high, mid], rub.at[low_ghost, mid], cs.at[1], cr.at[1])
+        halo(cw.at[7, 1, mid], cw.at[7, ncx + 1, mid], cw.at[7, ncx, mid], cw.at[7, 0, mid], cs.at[2], cr.at[2])
+
+    coarse_inputs()
 
     def fine_weights(plane):
         half = 0.5 * fine_step
@@ -213,7 +235,6 @@
     halo_wait(kb.at[nx + 1, inner], kb.at[0, inner], kr)
     fine_weights(0)
     fine_weights(nx - 1)
-    load_u.wait()
 
     def fine_plane(ref, plane, count, store):
         for at in range(0, count, CHUNK):
@@ -245,26 +266,6 @@
         def store(plane, at, size, value):
             ref[plane + 1, PAD + at:PAD + at + size] = value
         return store
-
-    def restrict_plane(ref, plane, base):
-        total = ref[plane, pl.ds(base, ncy, stride=2)] + ref[plane, pl.ds(base + 1, ncy, stride=2)]
-        total += ref[plane + 1, pl.ds(base, ncy, stride=2)]
-        total += ref[plane + 1, pl.ds(base + 1, ncy, stride=2)]
-        return total * 0.25
-
-    core = slice(side, side + ncy)
-    mid = pl.ds(side, ncy)
-
-    def coarse_inputs():
-        for plane in range(ncx):
-            rub[plane + 2, core] = restrict_plane(ub.at[0], 2 * plane + 1, PAD)
-            kcb[plane + 2, core] = restrict_plane(kb, 2 * plane + 1, PAD)
-            cw[7, plane + 1, core] = coarse_step * restrict_plane(src, 2 * plane, 0)
-        low, high = pl.ds(2, 2), pl.ds(ncx, 2)
-        low_ghost, high_ghost = pl.ds(0, 2), pl.ds(ncx + 2, 2)
-        halo(kcb.at[low, mid], kcb.at[high_ghost, mid], kcb.at[high, mid], kcb.at[low_ghost, mid], cs.at[0], cr.at[0])
-        halo(rub.at[low, mid], rub.at[high_ghost, mid], rub.at[high, mid], rub.at[low_ghost, mid], cs.at[1], cr.at[1])
-        halo(cw.at[7, 1, mid], cw.at[7, ncx + 1, mid], cw.at[7, ncx, mid], cw.at[7, 0, mid], cs.at[2], cr.at[2])
 
     def coarse_weights():
         low_ghost, high_ghost = pl.ds(0, 2), pl.ds(ncx + 2, 2)
@@ -321,10 +322,9 @@
                 send_fine(step + 1)
 
         sweep(ub.at[step], ny, into(ub.at[step + 1]), send)
-        if step == 0:
-            coarse_inputs()
+        if step == FSTEPS - 3:
+            coarse_weights()
         if step == FSTEPS - 2:
-            coarse_weights()
 
             def keep_minus(plane, value):
                 delta[plane] = jnp.where(tm > 0, -value, 0.0)
@@ -410,6 +410,7 @@
         for plane in range(ncx):
             ec[plane] = jnp.zeros((ncy, nz), jnp.float32)
 
+    stored = []
     for by in range(slabs):
         arrive(jnp.logical_and(tm != 1, tm != by), ec.at[:, pl.ds(rows * by, rows)], er.at[by])
     for pair in range(ncx):
@@ -418,10 +419,13 @@
         value = jnp.where(tm == 1, 0.0, value)
         tmp[pair, pl.ds(0, ncy, stride=2)] = value
         tmp[pair, pl.ds(1, ncy, stride=2)] = value
-        for at in range(0, ny, CHUNK):
-            q = slice(at, at + CHUNK)
-            out[2 * pair, q] = full[2 * pair, q] + tmp[pair, q]
-            out[2 * pair + 1, q] = full[2 * pair + 1, q] + tmp[pair, q]
+        put_lift = pltpu.make_async_copy(tmp.at[pair], lift.at[pair], put_sem.at[1, pair])
+        put_lift.start()
+        put_out = pltpu.make_async_copy(full.at[pl.ds(2 * pair, 2)], out.at[pl.ds(2 * pair, 2)], put_sem.at[0, pair])
+        put_out.start()
+        stored += [put_lift, put_out]
+    for copy in stored:
+        copy.wait()
     for cond, copy in pending:
         @pl.when(cond)
         def _(copy=copy):
@@ -436,7 +440,7 @@
     side = -(-CSTEPS * (slabs - 1) // 8) * 8
     whole = ncy + 2 * side
     width = ncy // slabs + 2 * side
-    early = ny * 5 // 64 * 8
+    early = ny * 6 // 64 * 8
     f32 = functools.partial(pltpu.VMEM, dtype=jnp.float32)
     sems = lambda *shape: pltpu.SemaphoreType.DMA(shape)
     field = (nx, ny, nz)
@@ -470,19 +474,20 @@
         sems(slabs), sems(slabs),
         sems(slabs), sems(slabs),
         sems(ncx), sems(ncx),
+        sems(2, ncx),
     ]
     hbm = pl.BlockSpec(memory_space=pl.ANY)
-    result = pl.pallas_call(
+    fine, lift = pl.pallas_call(
         functools.partial(kernel, slabs, blocks),
-        out_shape=jax.ShapeDtypeStruct(field, jnp.float32),
+        out_shape=[jax.ShapeDtypeStruct(field, jnp.float32), jax.ShapeDtypeStruct((ncx, ny, nz), jnp.float32)],
         in_specs=[hbm, hbm, hbm],
-        out_specs=pl.BlockSpec(memory_space=pltpu.VMEM),
+        out_specs=[hbm, hbm],
         scratch_shapes=scratch,
         compiler_params=pltpu.CompilerParams(
             collective_id=0, has_side_effects=True, vmem_limit_bytes=60 * 1024 * 1024
         ),
     )(starts, material, source)
-    return result[None]
+    return (fine.reshape(ncx, 2, ny, nz) + lift[:, None]).reshape(1, nx, ny, nz)
 
 
 def solution(mesh):

time: 52.8 us -> 46.9 us (0.89)
  Pallas kernels: 50 us -> 43.9 us
  other arithmetic: 0 us -> 2.42 us
  local copies, waits for them, and re-layouts: 2.27 us -> 0 us
    pallas_call x1, Pallas kernels: 50 us -> 43.9 us  [local(): pl.pallas_call(functools.partial(kernel, slabs, blocks), out_shape=[jax.S...]
    add x0 -> x1, other arithmetic: none -> 2.42 us  [local(): return (fine.reshape(ncx, 2, ny, nz) + lift[:, None]).reshape(1, nx, ny, nz)]
    unnamed x1 -> x0, local copies, waits for them, and re-layouts: 2.27 us -> none
where the time goes in v3:
time: 46.9 us; the launch traced here: 46.4 us
  Pallas kernels  43.9 us (94%)
  other arithmetic  2.42 us (5%)
    pallas_call x1, Pallas kernels, local(): pl.pallas_call(functools.partial(kernel, slabs, blocks), out_shape=[jax.S...  43.9 us
    add x1, other arithmetic, local(): return (fine.reshape(ncx, 2, ny, nz) + lift[:, None]).reshape(1, nx, ny, nz)  2.42 us

profile of v3, /device:TPU:1, one launch (start us, length us, event | category | flops | bytes accessed | tf_op | source)
XLA Modules:
  0.0 46.4 jit_solution(1029720085186787728)
XLA Ops:
  0.0 43.9 %shard_map.37 = (f32[8,256,128]{2,1,0:T(8,128)}, f32[4,256,128]{2,1,0:T(8,128)}) custom-call(f32[1,8,256,128]{3,2,1,0:T(8,128)} %starts.1, s32[8,256,128]{2,1,0:T(8,128)} %material.1, f32[8,256,128]{2,1,0:T(8,128)} %source.1), custom_call_target="tpu_custom_call" | custom-call | tf_op jit(solution)/shard_map/pallas_call | solution.py:480
  43.9 2.4 %bitcast_add_fusion = f32[8,256,128]{2,1,0:T(8,128)} fusion(f32[8,256,128]{2,1,0:T(8,128)} %get-tuple-element.7, f32[4,256,128]{2,1,0:T(8,128)} %get-tuple-element.8), kind=kLoop, calls=%fused_computation | loop fusion | flops 262144 | bytes 2621440 | tf_op jit(solution)/shard_map/add | solution.py:490

commit v4 on v3

--- a/solution.py
+++ b/solution.py
@@ -27,7 +27,7 @@
 
 
 def kernel(slabs, blocks, starts, material, source, out, lift, mat, src, ub, ub2, kb, wx, wyl, wyh, wzl, wzh, c0, hs, full,
-           kcb, cw, rub, rum, delta, rb, rm, got, last_state, ec, tmp, load_sem,
+           kcb, cw, rub, rum, delta, rb, rm, got, last_state, ec, ends, tmp, load_sem,
            fs, fr, f2s, f2r, ks, kr, cs, cr, chs, chr_, us, ur, vs, vr, es, er, bs, br, put_sem):
     nx, ny, nz = src.shape
     ncx, ncy = nx // 2, ny // 2
@@ -335,9 +335,6 @@
         delta[plane, core] = delta[plane, core] + restrict_plane(ub.at[FSTEPS], 2 * plane + 1, PAD)
     for to in range(slabs):
         remote(tm != to, delta.at[:, pl.ds(rows * to, width)], got.at[tm], vs.at[to], vr.at[tm], tm=to)
-    for pair in range(ncx):
-        remote(True, ub.at[FSTEPS, pl.ds(2 * pair + 1, 2), pl.ds(PAD + late, ny - late)],
-               full.at[pl.ds(2 * pair, 2), pl.ds(late, ny - late)], bs.at[pair], br.at[pair], tm=after)
 
     mine = pl.ds(pl.multiple_of(rows * tm, 8), width)
 
@@ -399,6 +396,9 @@
     for plane in range(ncx):
         rb[0, plane + 2] = got[0, plane]
     send_chain(0)
+    for pair in range(ncx):
+        remote(True, ub.at[FSTEPS, pl.ds(2 * pair + 1, 2), pl.ds(PAD + late, ny - late)],
+               full.at[pl.ds(2 * pair, 2), pl.ds(late, ny - late)], bs.at[pair], br.at[pair], tm=after)
     for turn in range(max(FSTEPS - 1, live)):
         if turn + 1 < FSTEPS:
             early_step(turn + 1)
@@ -411,19 +411,21 @@
             ec[plane] = jnp.zeros((ncy, nz), jnp.float32)
 
     stored = []
+    for pair in range(ncx):
+        arrive(True, full.at[pl.ds(2 * pair, 2), pl.ds(late, ny - late)], br.at[pair])
+        put_out = pltpu.make_async_copy(full.at[pl.ds(2 * pair, 2)], out.at[pl.ds(2 * pair, 2)], put_sem.at[0, pair])
+        put_out.start()
+        stored.append(put_out)
+        ends[pair] = restrict_plane(full, 2 * pair, 0)
     for by in range(slabs):
         arrive(jnp.logical_and(tm != 1, tm != by), ec.at[:, pl.ds(rows * by, rows)], er.at[by])
     for pair in range(ncx):
-        arrive(True, full.at[pl.ds(2 * pair, 2), pl.ds(late, ny - late)], br.at[pair])
-        value = ec[pair] - restrict_plane(full, 2 * pair, 0)
-        value = jnp.where(tm == 1, 0.0, value)
+        value = jnp.where(tm == 1, 0.0, ec[pair] - ends[pair])
         tmp[pair, pl.ds(0, ncy, stride=2)] = value
         tmp[pair, pl.ds(1, ncy, stride=2)] = value
         put_lift = pltpu.make_async_copy(tmp.at[pair], lift.at[pair], put_sem.at[1, pair])
         put_lift.start()
-        put_out = pltpu.make_async_copy(full.at[pl.ds(2 * pair, 2)], out.at[pl.ds(2 * pair, 2)], put_sem.at[0, pair])
-        put_out.start()
-        stored += [put_lift, put_out]
+        stored.append(put_lift)
     for copy in stored:
         copy.wait()
     for cond, copy in pending:
@@ -463,6 +465,7 @@
         f32((slabs, ncx, width, nz)),
         f32((ncx, width, nz)),
         f32((ncx, ncy, nz)),
+        f32((ncx, ncy, nz)),
         f32((ncx, ny, nz)),
         sems(3),
         sems(FSTEPS, 2), sems(FSTEPS, 2),

time: 46.9 us -> 46.5 us (level)
  the two profiles are of different devices: /device:TPU:1 before, /device:TPU:17 now
where the time goes in v4:
time: 46.5 us; the launch traced here: 46.4 us
  Pallas kernels  43.9 us (94%)
  other arithmetic  2.42 us (5%)
    pallas_call x1, Pallas kernels, local(): pl.pallas_call(functools.partial(kernel, slabs, blocks), out_shape=[jax.S...  43.9 us
    add x1, other arithmetic, local(): return (fine.reshape(ncx, 2, ny, nz) + lift[:, None]).reshape(1, nx, ny, nz)  2.42 us

profile of v4, /device:TPU:17, one launch (start us, length us, event | category | flops | bytes accessed | tf_op | source)
XLA Modules:
  0.0 46.4 jit_solution(914037965453052048)
XLA Ops:
  0.0 43.9 %shard_map.37 = (f32[8,256,128]{2,1,0:T(8,128)}, f32[4,256,128]{2,1,0:T(8,128)}) custom-call(f32[1,8,256,128]{3,2,1,0:T(8,128)} %starts.1, s32[8,256,128]{2,1,0:T(8,128)} %material.1, f32[8,256,128]{2,1,0:T(8,128)} %source.1), custom_call_target="tpu_custom_call" | custom-call | tf_op jit(solution)/shard_map/pallas_call | solution.py:483
  43.9 2.4 %bitcast_add_fusion = f32[8,256,128]{2,1,0:T(8,128)} fusion(f32[8,256,128]{2,1,0:T(8,128)} %get-tuple-element.7, f32[4,256,128]{2,1,0:T(8,128)} %get-tuple-element.8), kind=kLoop, calls=%fused_computation | loop fusion | flops 262144 | bytes 2621440 | tf_op jit(solution)/shard_map/add | solution.py:493
